TPU v7x, 32 devices: a whole 2x2x4 slice. The times are simulated.
32 devices in a mesh: fsdp: 32 (over z, y, x, core).
Axes of the slice: x: 2, y: 2, z: 4, core: 2. Of those that a mesh axis runs over, the one named last changes fastest.
Arguments:
- hidden_in: bfloat16 [16384, 1024], P('fsdp'), may hold values from -6 to 6
- cotangent: bfloat16 [16384, 1024], P('fsdp'), may hold values from -6 to 6
- segment_ids: int32 [16384], P('fsdp'), may hold values from 0 to 15, never falling along the last dimension, each value on 1 to 2048 neighbouring positions
- qkv_weight: bfloat16 [1024, 3072], P('fsdp'), may hold values from -0.1875 to 0.1875
- qkv_bias: bfloat16 [3072], P('fsdp'), may hold values from -1 to 1
- dense_weight: bfloat16 [1024, 1024], P('fsdp'), may hold values from -0.5 to 0.5
- dense_bias: bfloat16 [1024], P('fsdp'), may hold values from -1 to 1
- upper_weight: bfloat16 [1024, 4096], P('fsdp'), may hold values from -0.1875 to 0.1875
- upper_bias: bfloat16 [4096], P('fsdp'), may hold values from -1 to 1
- lower_weight: bfloat16 [4096, 1024], P('fsdp'), may hold values from -0.09375 to 0.09375
- lower_bias: bfloat16 [1024], P('fsdp'), may hold values from -1 to 1
- attn_norm_gain: bfloat16 [1024], P('fsdp'), may hold values from 0.5 to 1.5
- attn_norm_bias: bfloat16 [1024], P('fsdp'), may hold values from -1 to 1
- mlp_norm_gain: bfloat16 [1024], P('fsdp'), may hold values from 0.5 to 1.5
- mlp_norm_bias: bfloat16 [1024], P('fsdp'), may hold values from -1 to 1
Outputs:
- hidden_out: bfloat16 [16384, 1024], P('fsdp')
- hidden_grad: float32 [16384, 1024], P('fsdp')
- qkv_weight_grad: float32 [1024, 3072], P('fsdp')
- qkv_bias_grad: float32 [3072], P('fsdp')
- dense_weight_grad: float32 [1024, 1024], P('fsdp')
- dense_bias_grad: float32 [1024], P('fsdp')
- upper_weight_grad: float32 [1024, 4096], P('fsdp')
- upper_bias_grad: float32 [4096], P('fsdp')
- lower_weight_grad: float32 [4096, 1024], P('fsdp')
- lower_bias_grad: float32 [1024], P('fsdp')
- attn_norm_gain_grad: float32 [1024], P('fsdp')
- attn_norm_bias_grad: float32 [1024], P('fsdp')
- mlp_norm_gain_grad: float32 [1024], P('fsdp')
- mlp_norm_bias_grad: float32 [1024], P('fsdp')
Inputs may be any that keep to these rules, and one draw needn't show every extreme that they name: `segment_ids`: Non-decreasing along the tokens; every number from 0 to 15 names one sequence of 1 to 2048 consecutive tokens, and some sequence has exactly 2048 tokens.
All inputs are finite; a program needn't handle non-finite values.
Results may differ from a plain program's by a relative error of at most 0.0085.
Values may be sent and summed in bfloat16 or wider, within the bound.
A program may use at most 256 MiB of HBM per device.

v0:
```python
from functools import partial

import jax
import jax.numpy as jnp
from jax import lax
from jax.sharding import PartitionSpec as P

HEAD_DIM = 64
ROT = 16
LMAX = 2048


norm_eps = 1e-05
masked_score = -1e30


def shifted(block, axis, distance):
    devices = range(lax.axis_size(axis))
    route = [(i - distance, i) for i in devices if i - distance in devices]
    return lax.ppermute(block, axis, route)


def layer_norm(values_in, gain_row, shift_row):
    mean_value = jnp.mean(values_in, axis=-1, keepdims=True)
    centred = values_in - mean_value
    variance = jnp.mean(centred * centred, axis=-1, keepdims=True)
    inverse = lax.rsqrt(variance + norm_eps)
    normal = centred * inverse
    return (normal * gain_row + shift_row, normal, inverse)


def norm_back(gradient, normal, inverse, gain_row):
    inner_sum = gradient * gain_row
    centred = inner_sum - jnp.mean(inner_sum, axis=-1, keepdims=True)
    return inverse * (centred - normal * jnp.mean(inner_sum * normal, axis=-1, keepdims=True))


def rotary_tables(positions):
    inverse = 10000.0 ** (-jnp.arange(0, ROT, 2, dtype=jnp.float32) / ROT)
    angles = positions.astype(jnp.float32)[:, None] * inverse[None, :]
    angles = jnp.concatenate([angles, angles], axis=-1)
    return (jnp.cos(angles), jnp.sin(angles))


def rotate(values_in, cos_table, sin_table):
    middle = ROT // 2
    portion = values_in[..., :ROT]
    turned = jnp.concatenate([-portion[..., middle:], portion[..., :middle]], axis=-1)
    rotated = portion * cos_table[:, None, :] + turned * sin_table[:, None, :]
    return jnp.concatenate([rotated, values_in[..., ROT:]], axis=-1)


def rotate_back(gradient, cos_table, sin_table):
    middle = ROT // 2
    portion = gradient[..., :ROT]
    scaled_part = portion * sin_table[:, None, :]
    turned = jnp.concatenate([scaled_part[..., middle:], -scaled_part[..., :middle]], axis=-1)
    return jnp.concatenate([portion * cos_table[:, None, :] + turned, gradient[..., ROT:]], axis=-1)


def by_heads(flat_rows, head_count):
    return flat_rows.reshape(flat_rows.shape[0], head_count, HEAD_DIM).transpose(1, 0, 2)


def block_mask(query_segment, key_segment):
    row_index = jnp.arange(query_segment.shape[0])[:, None]
    column_index = jnp.arange(key_segment.shape[0])[None, :]
    return (query_segment[:, None] == key_segment[None, :]) & (column_index <= row_index + LMAX)


def head_forward(operands, allowed, score_scale):
    queries, keys, values_in = operands
    scores = (
        jnp.einsum("qd,kd->qk", queries, keys, preferred_element_type=jnp.float32) * score_scale
    )
    scores = jnp.where(allowed, scores, masked_score)
    maximum = jnp.max(scores, axis=-1, keepdims=True)
    exponent = jnp.exp(scores - maximum)
    totals = jnp.sum(exponent, axis=-1, keepdims=True)
    probabilities = (exponent / totals).astype(jnp.bfloat16)
    attended = jnp.dot(probabilities, values_in, preferred_element_type=jnp.float32)
    return (attended, (maximum + jnp.log(totals))[:, 0])


def head_backward(operands, allowed, score_scale):
    queries, keys, values_in, grad_out, log_totals = operands
    scores = (
        jnp.einsum("qd,kd->qk", queries, keys, preferred_element_type=jnp.float32) * score_scale
    )
    scores = jnp.where(allowed, scores, masked_score)
    probabilities = jnp.exp(scores - log_totals[:, None])
    grad_probs = jnp.einsum("qd,kd->qk", grad_out, values_in, preferred_element_type=jnp.float32)
    inner_sum = jnp.sum(probabilities * grad_probs, axis=-1, keepdims=True)
    grad_scores = (probabilities * (grad_probs - inner_sum)).astype(jnp.bfloat16)
    grad_queries = jnp.dot(grad_scores, keys, preferred_element_type=jnp.float32) * score_scale
    grad_keys = (
        jnp.einsum("qk,qd->kd", grad_scores, queries, preferred_element_type=jnp.float32)
        * score_scale
    )
    grad_values = jnp.einsum(
        "qk,qd->kd",
        probabilities.astype(jnp.bfloat16),
        grad_out,
        preferred_element_type=jnp.float32,
    )
    return (grad_queries, grad_keys, grad_values)


def on_device(
    hidden_in,
    cotangent,
    segment_ids,
    qkv_weight,
    qkv_bias,
    dense_weight,
    dense_bias,
    upper_weight,
    upper_bias,
    lower_weight,
    lower_bias,
    attn_norm_gain,
    attn_norm_bias,
    mlp_norm_gain,
    mlp_norm_bias,
):
    shards = (
        qkv_weight,
        qkv_bias,
        dense_weight,
        dense_bias,
        upper_weight,
        upper_bias,
        lower_weight,
        lower_bias,
        attn_norm_gain,
        attn_norm_bias,
        mlp_norm_gain,
        mlp_norm_bias,
    )
    gathered = (
        lax.all_gather(shards[0], "fsdp", axis=0, tiled=True),
        lax.all_gather(shards[1], "fsdp", axis=0, tiled=True),
        lax.all_gather(shards[2], "fsdp", axis=0, tiled=True),
        lax.all_gather(shards[3], "fsdp", axis=0, tiled=True),
        lax.all_gather(shards[4], "fsdp", axis=0, tiled=True),
        lax.all_gather(shards[5], "fsdp", axis=0, tiled=True),
        lax.all_gather(shards[6], "fsdp", axis=0, tiled=True),
        lax.all_gather(shards[7], "fsdp", axis=0, tiled=True),
        lax.all_gather(shards[8], "fsdp", axis=0, tiled=True),
        lax.all_gather(shards[9], "fsdp", axis=0, tiled=True),
        lax.all_gather(shards[10], "fsdp", axis=0, tiled=True),
        lax.all_gather(shards[11], "fsdp", axis=0, tiled=True),
    )
    local_rows = hidden_in.shape[0]
    features = hidden_in.shape[1]
    head_count = features // HEAD_DIM
    reach_devices = -(-LMAX // local_rows)
    block_rows = min(512, local_rows)
    window = block_rows + LMAX
    offset = reach_devices * local_rows
    score_scale = HEAD_DIM ** (-0.5)
    segment_plus = segment_ids + 1
    earlier = [shifted(segment_plus, "fsdp", distance) for distance in range(reach_devices, 0, -1)]
    ext_segment = jnp.concatenate(earlier + [segment_plus])
    below_count = jnp.sum((ext_segment[None, :] < segment_plus[:, None]).astype(jnp.int32), axis=1)
    positions = jnp.arange(local_rows, dtype=jnp.int32) + offset - below_count
    cos_table, sin_table = rotary_tables(positions)
    hidden_f = hidden_in.astype(jnp.float32)
    normed_attn, normal_attn, inverse_attn = layer_norm(
        hidden_f, gathered[8].astype(jnp.float32), gathered[9].astype(jnp.float32)
    )
    normed_attn = normed_attn.astype(jnp.bfloat16)
    projected = jnp.dot(normed_attn, gathered[0], preferred_element_type=jnp.float32) + gathered[
        1
    ].astype(jnp.float32)
    query_pre = projected[:, :features].reshape(local_rows, head_count, HEAD_DIM)
    key_pre = projected[:, features : 2 * features].reshape(local_rows, head_count, HEAD_DIM)
    query_rot = rotate(query_pre, cos_table, sin_table).astype(jnp.bfloat16)
    key_rot = (
        rotate(key_pre, cos_table, sin_table).astype(jnp.bfloat16).reshape(local_rows, features)
    )
    value_low = projected[:, 2 * features :].astype(jnp.bfloat16)
    fetched = [
        shifted((key_rot, value_low), "fsdp", distance) for distance in range(reach_devices, 0, -1)
    ]
    ext_keys = jnp.concatenate([fetched_pair[0] for fetched_pair in fetched] + [key_rot])
    ext_values = jnp.concatenate([fetched_pair[1] for fetched_pair in fetched] + [value_low])
    key_heads = by_heads(ext_keys, head_count)
    value_heads = by_heads(ext_values, head_count)
    query_heads = query_rot.transpose(1, 0, 2)
    allowed = block_mask(segment_plus, ext_segment)
    head_out, head_totals = lax.map(
        partial(head_forward, allowed=allowed, score_scale=score_scale),
        (query_heads, key_heads, value_heads),
    )
    attended = head_out.transpose(1, 0, 2).reshape(local_rows, features)
    attended = attended.astype(jnp.bfloat16)
    attn_branch = jnp.dot(attended, gathered[2], preferred_element_type=jnp.float32) + gathered[
        3
    ].astype(jnp.float32)
    normed_mlp, normal_mlp, inverse_mlp = layer_norm(
        hidden_f, gathered[10].astype(jnp.float32), gathered[11].astype(jnp.float32)
    )
    normed_mlp = normed_mlp.astype(jnp.bfloat16)
    upper = jnp.dot(normed_mlp, gathered[4], preferred_element_type=jnp.float32) + gathered[
        5
    ].astype(jnp.float32)
    gelu_exact = partial(jax.nn.gelu, approximate=False)
    active, gelu_pull = jax.vjp(gelu_exact, upper)
    active = active.astype(jnp.bfloat16)
    mlp_branch = jnp.dot(active, gathered[6], preferred_element_type=jnp.float32) + gathered[
        7
    ].astype(jnp.float32)
    hidden_out = (hidden_f + attn_branch + mlp_branch).astype(jnp.bfloat16)
    again = (
        lax.all_gather(shards[0], "fsdp", axis=0, tiled=True),
        lax.all_gather(shards[1], "fsdp", axis=0, tiled=True),
        lax.all_gather(shards[2], "fsdp", axis=0, tiled=True),
        lax.all_gather(shards[3], "fsdp", axis=0, tiled=True),
        lax.all_gather(shards[4], "fsdp", axis=0, tiled=True),
        lax.all_gather(shards[5], "fsdp", axis=0, tiled=True),
        lax.all_gather(shards[6], "fsdp", axis=0, tiled=True),
        lax.all_gather(shards[7], "fsdp", axis=0, tiled=True),
        lax.all_gather(shards[8], "fsdp", axis=0, tiled=True),
        lax.all_gather(shards[9], "fsdp", axis=0, tiled=True),
        lax.all_gather(shards[10], "fsdp", axis=0, tiled=True),
        lax.all_gather(shards[11], "fsdp", axis=0, tiled=True),
    )
    qkv_full = again[0]
    dense_full = again[2]
    upper_full = again[4]
    lower_full = again[6]
    gain_attn = again[8].astype(jnp.float32)
    gain_mlp = again[10].astype(jnp.float32)
    cotangent_f = cotangent.astype(jnp.float32)
    lower_weight_grad = jnp.einsum(
        "tf,td->fd", active, cotangent, preferred_element_type=jnp.float32
    )
    dense_weight_grad = jnp.einsum(
        "te,td->ed", attended, cotangent, preferred_element_type=jnp.float32
    )
    column_sums = jnp.sum(cotangent_f, axis=0)
    grad_active = jnp.einsum("td,fd->tf", cotangent, lower_full, preferred_element_type=jnp.float32)
    grad_upper = gelu_pull(grad_active)[0].astype(jnp.bfloat16)
    upper_weight_grad = jnp.einsum(
        "td,tf->df", normed_mlp, grad_upper, preferred_element_type=jnp.float32
    )
    upper_bias_grad = jnp.sum(grad_upper.astype(jnp.float32), axis=0)
    grad_norm_mlp = jnp.einsum(
        "tf,df->td", grad_upper, upper_full, preferred_element_type=jnp.float32
    )
    mlp_gain_grad = jnp.sum(grad_norm_mlp * normal_mlp, axis=0)
    mlp_shift_grad = jnp.sum(grad_norm_mlp, axis=0)
    grad_attended = jnp.einsum(
        "te,de->td", cotangent, dense_full, preferred_element_type=jnp.float32
    )
    grad_heads = by_heads(grad_attended.astype(jnp.bfloat16), head_count)
    ext_rows = offset + local_rows
    grad_keys = jnp.zeros((head_count, ext_rows, HEAD_DIM), jnp.float32)
    grad_values = jnp.zeros((head_count, ext_rows, HEAD_DIM), jnp.float32)
    window_start = offset - LMAX
    allowed = block_mask(segment_plus, ext_segment)
    grad_query_block, grad_key_block, grad_value_block = lax.map(
        partial(head_backward, allowed=allowed, score_scale=score_scale),
        (query_heads, key_heads, value_heads, grad_heads, head_totals),
    )
    grad_keys = grad_keys.at[:, window_start : window_start + window].add(grad_key_block)
    grad_values = grad_values.at[:, window_start : window_start + window].add(grad_value_block)
    grad_keys = grad_keys.transpose(1, 0, 2).reshape(ext_rows, features)
    grad_values = grad_values.transpose(1, 0, 2).reshape(ext_rows, features)
    own_keys = grad_keys[offset:]
    own_values = grad_values[offset:]

    def earlier_rows(array_rows, distance):
        return array_rows[offset - distance * local_rows : offset - (distance - 1) * local_rows]

    for distance in range(1, reach_devices + 1):
        returned = shifted(
            (earlier_rows(grad_keys, distance), earlier_rows(grad_values, distance)),
            "fsdp",
            -distance,
        )
        own_keys = own_keys + returned[0]
        own_values = own_values + returned[1]
    grad_query = grad_query_block.transpose(1, 0, 2)
    grad_query = (
        rotate_back(grad_query, cos_table, sin_table)
        .astype(jnp.bfloat16)
        .reshape(local_rows, features)
    )
    grad_key = rotate_back(own_keys.reshape(local_rows, head_count, HEAD_DIM), cos_table, sin_table)
    grad_key = grad_key.astype(jnp.bfloat16).reshape(local_rows, features)
    grad_value = own_values.astype(jnp.bfloat16)
    grad_qkv = jnp.concatenate([grad_query, grad_key, grad_value], axis=1)
    qkv_weight_grad = jnp.einsum(
        "td,tj->dj", normed_attn, grad_qkv, preferred_element_type=jnp.float32
    )
    qkv_bias_grad = jnp.sum(grad_qkv.astype(jnp.float32), axis=0)
    grad_norm_attn = jnp.einsum("tj,dj->td", grad_qkv, qkv_full, preferred_element_type=jnp.float32)
    attn_gain_grad = jnp.sum(grad_norm_attn * normal_attn, axis=0)
    attn_shift_grad = jnp.sum(grad_norm_attn, axis=0)
    hidden_grad = (
        cotangent_f
        + norm_back(grad_norm_attn, normal_attn, inverse_attn, gain_attn)
        + norm_back(grad_norm_mlp, normal_mlp, inverse_mlp, gain_mlp)
    )
    summed = (
        lax.psum_scatter(qkv_weight_grad, "fsdp", scatter_dimension=0, tiled=True),
        lax.psum_scatter(qkv_bias_grad, "fsdp", scatter_dimension=0, tiled=True),
        lax.psum_scatter(dense_weight_grad, "fsdp", scatter_dimension=0, tiled=True),
        lax.psum_scatter(column_sums, "fsdp", scatter_dimension=0, tiled=True),
        lax.psum_scatter(upper_weight_grad, "fsdp", scatter_dimension=0, tiled=True),
        lax.psum_scatter(upper_bias_grad, "fsdp", scatter_dimension=0, tiled=True),
        lax.psum_scatter(lower_weight_grad, "fsdp", scatter_dimension=0, tiled=True),
        lax.psum_scatter(column_sums, "fsdp", scatter_dimension=0, tiled=True),
        lax.psum_scatter(attn_gain_grad, "fsdp", scatter_dimension=0, tiled=True),
        lax.psum_scatter(attn_shift_grad, "fsdp", scatter_dimension=0, tiled=True),
        lax.psum_scatter(mlp_gain_grad, "fsdp", scatter_dimension=0, tiled=True),
        lax.psum_scatter(mlp_shift_grad, "fsdp", scatter_dimension=0, tiled=True),
    )
    return (
        hidden_out,
        hidden_grad,
        summed[0],
        summed[1],
        summed[2],
        summed[3],
        summed[4],
        summed[5],
        summed[6],
        summed[7],
        summed[8],
        summed[9],
        summed[10],
        summed[11],
    )


def solution(mesh):
    placed = (
        P("fsdp", None),
        P("fsdp", None),
        P("fsdp"),
        P("fsdp", None),
        P("fsdp"),
        P("fsdp", None),
        P("fsdp"),
        P("fsdp", None),
        P("fsdp"),
        P("fsdp", None),
        P("fsdp"),
        P("fsdp"),
        P("fsdp"),
        P("fsdp"),
        P("fsdp"),
    )
    return jax.shard_map(
        on_device,
        mesh=mesh,
        in_specs=placed,
        out_specs=(
            P("fsdp", None),
            P("fsdp", None),
            P("fsdp", None),
            P("fsdp"),
            P("fsdp", None),
            P("fsdp"),
            P("fsdp", None),
            P("fsdp"),
            P("fsdp", None),
            P("fsdp"),
            P("fsdp"),
            P("fsdp"),
            P("fsdp"),
            P("fsdp"),
        ),
        check_vma=False,
    )
```

profile of v0, /device:TPU:0, one launch (start us, length us, event | category | flops | bytes accessed | tf_op | source)
XLA Modules:
  0.0 1674.8 jit_solution(5539202082002783842)
XLA Ops:
  10.1 4.9 collective-permute-start
  17.6 3.4 collective-permute-start.2
  32.6 41.6 %all-reduce.15 = (bf16[1024]{0:T(1024)(128)(2,1)}, bf16[1024]{0:T(1024)(128)(2,1)}, bf16[3072]{0:T(1024)(128)(2,1)S(1)}, bf16[1024]{0:T(1024)(128)(2,1)S(1)}, bf...) all-reduce(bf16[1024]{0:T(1024)(128)(2,1)S(1)} %dynamic-update-slic, ...), channel_id=1, replica_groups=mesh['fsdp'=32] {'fsdp'}, use_global_device_ids=true, to_apply=%add.5 | all-reduce | flops 9216 | bytes 36864
  75.9 8.1 all-gather.6.cloned.1.call-done
  84.0 6.1 convolution_add_fusion
  102.3 4.4 collective-permute-start.4
  110.7 4.5 collective-permute-start.6
  117.5 69.3 %all-gather.8.cloned.1.call-done = bf16[1024,1024]{1,0:T(8,128)(2,1)} async-done(((bf16[32,1024]{1,0:T(8,128)(2,1)}), bf16[1024,1024]{1,0:T(8,128)(2,1)}) %all-gather.8.cloned.1.call-update) | async-done | bytes 2097168 | tf_op jit(solution)/shard_map/all_gather | solution.py:143
  186.8 4.2 convolution_convert_fusion
  196.0 3.5 collective-permute-start.8
  207.4 5.4 collective-permute-start.10
  226.8 10.2 copy.67
  237.0 34.0 %collective-permute-done.8 = bf16[512,1024]{1,0:T(8,128)(2,1)} collective-permute-done((bf16[512,1024]{1,0:T(8,128)(2,1)}, bf16[512,1024]{1,0:T(8,128)(2,1)}, u32[]{:S(2)}, u32[]{:S(2)}) %collective-permute-start.8) | collective-permute-done | bytes 1048608 | tf_op jit(solution)/shard_map/ppermute | solution.py:20
  281.8 7.7 copy.65
  289.5 10.3 copy.68
  299.8 155.9 %while.34 = (s32[]{:T(128)}, bf16[16,512,64]{1,2,0:T(8,128)(2,1)S(1)}, f32[16,512]{1,0:T(8,128)S(1)}, bf16[16,512,64]{2,1,0:T(8,128)(2,1)}, bf16[16,2560,64]{2,1...) while((s32[]{:T(128)}, ...), condition=%wide.region_6.7_spmd.clone.clone, body=%wide.region_3.6_spmd.clone.sunk.clone | while | flops 349961728 | bytes 38310012 | solution.py:192
  305.8 3.8 fusion.164
  315.5 3.8 fusion.164
  325.2 3.8 fusion.164
  335.0 3.8 fusion.164
  344.7 3.8 fusion.164
  354.4 3.8 fusion.164
  364.2 3.8 fusion.164
  373.9 3.9 fusion.164
  383.7 3.8 fusion.164
  393.6 3.8 fusion.164
  403.3 3.8 fusion.164
  413.0 3.8 fusion.164
  422.7 3.8 fusion.164
  432.5 3.8 fusion.164
  442.2 3.8 fusion.164
  451.9 3.8 fusion.164
  456.7 4.7 fusion.107
  461.5 201.1 %while.35 = (s32[]{:T(128)}, f32[16,512,64]{1,2,0:T(8,128)S(1)}, f32[16,2560,64]{1,2,0:T(8,128)}, f32[16,2560,64]{1,2,0:T(8,128)}, bf16[16,512,64]{2,1,0:T(8,128...) while((s32[]{:T(128)}, f32[16,512,64]{1,2,0:T(8,128)S(1)}, ...), condition=%wide.region_9.10_spmd.clone.clone, body=%wide.region_7.9_spmd.clone.sunk.clone | while | flops 854785536 | bytes 43152504 | solution.py:263
  463.5 3.4 multiply_reduce_fusion.5
  488.6 3.4 multiply_reduce_fusion.5
  513.8 3.4 multiply_reduce_fusion.5
  538.9 3.4 multiply_reduce_fusion.5
  564.0 3.4 multiply_reduce_fusion.5
  576.6 3.4 multiply_reduce_fusion.5
  589.2 3.4 multiply_reduce_fusion.5
  601.7 3.4 multiply_reduce_fusion.5
  614.3 3.4 multiply_reduce_fusion.5
  627.0 3.4 multiply_reduce_fusion.5
  639.5 3.4 multiply_reduce_fusion.5
  662.7 10.2 fusion.100
  678.7 4.1 fusion.101
  684.0 18.2 %collective-permute-done.12 = f32[512,1024]{0,1:T(8,128)} collective-permute-done((f32[512,1024]{0,1:T(8,128)}, f32[512,1024]{0,1:T(8,128)}, u32[]{:S(2)}, u32[]{:S(2)}) %collective-permute-start.12) | collective-permute-done | bytes 2097184 | tf_op jit(solution)/shard_map/ppermute | solution.py:20
  703.5 86.7 %collective-permute-done.13 = f32[512,1024]{0,1:T(8,128)} collective-permute-done((f32[512,1024]{0,1:T(8,128)}, f32[512,1024]{0,1:T(8,128)}, u32[]{:S(2)}, u32[]{:S(2)}) %collective-permute-start.13) | collective-permute-done | bytes 2097184 | tf_op jit(solution)/shard_map/ppermute | solution.py:20
  795.8 5.5 fusion.82
  802.5 77.4 %collective-permute-done.17 = f32[512,1024]{0,1:T(8,128)S(1)} collective-permute-done((f32[512,1024]{0,1:T(8,128)}, f32[512,1024]{0,1:T(8,128)S(1)}, u32[]{:S(2)}, u32[]{:S(2)}) %collective-permute-start.17) | collective-permute-done | bytes 2097184 | tf_op jit(solution)/shard_map/ppermute | solution.py:20
  883.7 9.6 fusion.94
  894.0 280.1 %all-gather = bf16[32,1,128]{2,1,0:T(2,128)(2,1)S(1)} all-gather(bf16[1,1,128]{2,1,0:T(2,128)(2,1)S(1)} %bitcast.216), channel_id=1, replica_groups=mesh['fsdp'=32] {'fsdp'}, dimensions={0}, use_global_device_ids=true | all-gather | bytes 8448 | tf_op jit(solution)/shard_map/all_gather | solution.py:146
  1174.2 10.9 fusion.92
  1185.1 27.7 %convert_reduce_fusion = (f32[4096]{0:T(1024)S(1)}, bf16[512,4096]{1,0:T(8,128)(2,1)}, f32[512,4096]{1,0:T(8,128)}) fusion(f32[512,4096]{1,0:T(8,128)} %fusion.92, f32[4096]{0:T(1024)S(1)} %bitcast.213, bf16[512,1024]{1,0:T(8,128)(2,1)S(1)} %copy-done.13, bf16[4096,1024]{1,0:T(8,128)(2,1)} %all-gather.12.cloned.1.call-done), kind=kOutput, calls=%fused_computation.57 | convolution fusion | flops 4452249600 | bytes 30441472 | tf_op jit(solution)/shard_map/td,fd->tf/dot_general | solution.py:243
  1212.8 10.0 multiply_convert_fusion.1
  1222.8 10.6 fusion.108
  1233.5 10.8 fusion.90
  1247.9 9.0 fusion.106
  1256.9 7.7 fusion.71
  1267.1 38.7 %all-reduce.14 = (f32[3072]{0:T(1024)S(1)}, f32[1024]{0:T(1024)S(1)}, f32[4096]{0:T(1024)S(1)}, f32[1024]{0:T(1024)S(1)}, f32[1024]{0:T(1024)S(1)}, /*index=5*/f32[1024]{0:T(1024)S(1)}, f32[1024]{0:T(1024)S(1)}) all-reduce(f32[3072]{0:T(1024)S(1)} %convert_reduce_fusion.1, ...), channel_id=3, replica_groups=mesh['fsdp'=32] {'fsdp'}, use_global_device_ids=true, to_apply=%region_16.17.clone | all-reduce | flops 12288 | bytes 98304
  1309.5 8.5 fusion.105
  1320.3 159.2 %reduce-scatter.11.cloned.1.call-done = f32[128,1024]{1,0:T(8,128)} async-done(((f32[4096,1024]{1,0:T(8,128)}), f32[128,1024]{1,0:T(8,128)}) %reduce-scatter.11.cloned.1.call-update) | async-done | bytes 524304 | tf_op jit(solution)/shard_map/reduce_scatter | solution.py:314
  1479.5 187.5 %reduce-scatter.9.cloned.1.call-done = f32[32,4096]{1,0:T(8,128)} async-done(((f32[1024,4096]{1,0:T(8,128)}), f32[32,4096]{1,0:T(8,128)}) %reduce-scatter.9.cloned.1.call-update) | async-done | bytes 524304 | tf_op jit(solution)/shard_map/reduce_scatter | solution.py:312
  (417 shorter events, 365.8 us)
Async XLA Ops:
  7.2 76.8 %all-gather.6.cloned.1.call-start = ((), (), s32[]{:S(2)}) async-start(), calls=%async_computation.4 | async-start | bytes 6488064 | tf_op jit(solution)/shard_map/all_gather | solution.py:141
  7.9 178.9 %all-gather.8.cloned.1.call-start = ((), (), s32[]{:S(2)}) async-start(), calls=%async_computation.5 | async-start | bytes 2162688 | tf_op jit(solution)/shard_map/all_gather | solution.py:143
  8.7 1165.5 %all-gather.10.cloned.1.call-start = ((), (), s32[]{:S(2)}) async-start(), calls=%async_computation.6 | async-start | bytes 8650752 | tf_op jit(solution)/shard_map/all_gather | solution.py:145
  9.4 1175.7 %all-gather.12.cloned.1.call-start = ((), (), s32[]{:S(2)}) async-start(), calls=%async_computation.7 | async-start | bytes 8650752 | tf_op jit(solution)/shard_map/all_gather | solution.py:147
  10.1 64.1 %collective-permute-start = (s32[512]{0:T(512)S(1)}, s32[512]{0:T(512)S(1)}, u32[]{:S(2)}, u32[]{:S(2)}) collective-permute-start(s32[512]{0:T(512)S(1)} %broadcast_add_fusion), channel_id=1, source_target_pairs={{0,4},{1,5},{2,6},{3,7},{4,8},{5,9},{6,10},{7,11},{8,12},{9,13},{1... | collective-permute-start | bytes 6152 | tf_op jit(solution)/shard_map/ppermute | solution.py:20
  15.0 59.2 %collective-permute-start.1 = (s32[512]{0:T(512)S(1)}, s32[512]{0:T(512)S(1)}, u32[]{:S(2)}, u32[]{:S(2)}) collective-permute-start(s32[512]{0:T(512)S(1)} %broadcast_add_fusion), channel_id=1, source_target_pairs={{0,3},{1,4},{2,5},{3,6},{4,7},{5,8},{6,9},{7,10},{8,11},{9,12},{10... | collective-permute-start | bytes 6152 | tf_op jit(solution)/shard_map/ppermute | solution.py:20
  17.6 56.7 %collective-permute-start.2 = (s32[512]{0:T(512)S(1)}, s32[512]{0:T(512)S(1)}, u32[]{:S(2)}, u32[]{:S(2)}) collective-permute-start(s32[512]{0:T(512)S(1)} %broadcast_add_fusion), channel_id=1, source_target_pairs={{0,2},{1,3},{2,4},{3,5},{4,6},{5,7},{6,8},{7,9},{8,10},{9,11},{10,... | collective-permute-start | bytes 6152 | tf_op jit(solution)/shard_map/ppermute | solution.py:20
  21.0 53.3 %collective-permute-start.3 = (s32[512]{0:T(512)S(1)}, s32[512]{0:T(512)S(1)}, u32[]{:S(2)}, u32[]{:S(2)}) collective-permute-start(s32[512]{0:T(512)S(1)} %broadcast_add_fusion), channel_id=1, source_target_pairs={{0,1},{1,2},{2,3},{3,4},{4,5},{5,6},{6,7},{7,8},{8,9},{9,10},{10,1... | collective-permute-start | bytes 6152 | tf_op jit(solution)/shard_map/ppermute | solution.py:20
  25.1 58.9 %copy-start.22 = (f32[512]{0:T(512)}, f32[512]{0:T(512)S(1)}, u32[]{:S(2)}) copy-start(f32[512]{0:T(512)S(1)} %broadcast_multiply_fusion.5) | copy-start | bytes 6148
  26.7 57.2 %copy-start.26 = (f32[512]{0:T(512)}, f32[512]{0:T(512)S(1)}, u32[]{:S(2)}) copy-start(f32[512]{0:T(512)S(1)} %add_rsqrt_fusion) | copy-start | bytes 6148
  74.2 9.8 copy-start.24
  74.2 9.8 copy-start.28
  75.9 128.8 %copy-start.18 = (f32[512,16]{0,1:T(8,128)}, f32[512,16]{0,1:T(8,128)S(1)}, u32[]{:S(2)}) copy-start(f32[512,16]{0,1:T(8,128)S(1)} %get-tuple-element.368) | copy-start | bytes 98308
  75.9 128.8 %copy-start.20 = (f32[512,16]{0,1:T(8,128)}, f32[512,16]{0,1:T(8,128)S(1)}, u32[]{:S(2)}) copy-start(f32[512,16]{0,1:T(8,128)S(1)} %get-tuple-element.367) | copy-start | bytes 98308
  90.1 2.7 copy-start.2
  102.3 100.1 %collective-permute-start.4 = (bf16[512,1024]{0,1:T(8,128)(2,1)}, bf16[512,1024]{0,1:T(8,128)(2,1)}, u32[]{:S(2)}, u32[]{:S(2)}) collective-permute-start(bf16[512,1024]{0,1:T(8,128)(2,1)} %bitcast.3), channel_id=1, source_target_pairs={{0,4},{1,5},{2,6},{3,7},{4,8},{5,9},{6,10},{7,11},{8,12},{9,13},{1... | collective-permute-start | bytes 3145736 | tf_op jit(solution)/shard_map/ppermute | solution.py:20
  106.7 1213.6 %reduce-scatter.7.cloned.1.call-start = ((), (), s32[]{:S(2)}) async-start(), calls=%async_computation.9 | async-start | bytes 4325376 | tf_op jit(solution)/shard_map/reduce_scatter | solution.py:310
  106.8 100.6 %collective-permute-start.5 = (bf16[512,1024]{0,1:T(8,128)(2,1)}, bf16[512,1024]{0,1:T(8,128)(2,1)}, u32[]{:S(2)}, u32[]{:S(2)}) collective-permute-start(bf16[512,1024]{0,1:T(8,128)(2,1)} %bitcast.3), channel_id=1, source_target_pairs={{0,3},{1,4},{2,5},{3,6},{4,7},{5,8},{6,9},{7,10},{8,11},{9,12},{10... | collective-permute-start | bytes 3145736 | tf_op jit(solution)/shard_map/ppermute | solution.py:20
  110.7 103.9 %collective-permute-start.6 = (bf16[512,1024]{0,1:T(8,128)(2,1)}, bf16[512,1024]{0,1:T(8,128)(2,1)}, u32[]{:S(2)}, u32[]{:S(2)}) collective-permute-start(bf16[512,1024]{0,1:T(8,128)(2,1)} %bitcast.3), channel_id=1, source_target_pairs={{0,2},{1,3},{2,4},{3,5},{4,6},{5,7},{6,8},{7,9},{8,10},{9,11},{10,... | collective-permute-start | bytes 3145736 | tf_op jit(solution)/shard_map/ppermute | solution.py:20
  115.2 108.1 %collective-permute-start.7 = (bf16[512,1024]{0,1:T(8,128)(2,1)}, bf16[512,1024]{0,1:T(8,128)(2,1)}, u32[]{:S(2)}, u32[]{:S(2)}) collective-permute-start(bf16[512,1024]{0,1:T(8,128)(2,1)} %bitcast.3), channel_id=1, source_target_pairs={{0,1},{1,2},{2,3},{3,4},{4,5},{5,6},{6,7},{7,8},{8,9},{9,10},{10,1... | collective-permute-start | bytes 3145736 | tf_op jit(solution)/shard_map/ppermute | solution.py:20
  196.0 75.1 %collective-permute-start.8 = (bf16[512,1024]{1,0:T(8,128)(2,1)}, bf16[512,1024]{1,0:T(8,128)(2,1)}, u32[]{:S(2)}, u32[]{:S(2)}) collective-permute-start(bf16[512,1024]{1,0:T(8,128)(2,1)} %slice.251), channel_id=1, source_target_pairs={{0,4},{1,5},{2,6},{3,7},{4,8},{5,9},{6,10},{7,11},{8,12},{9,13},{1... | collective-permute-start | bytes 3145736 | tf_op jit(solution)/shard_map/ppermute | solution.py:20
  202.4 71.0 %collective-permute-start.9 = (bf16[512,1024]{1,0:T(8,128)(2,1)}, bf16[512,1024]{1,0:T(8,128)(2,1)}, u32[]{:S(2)}, u32[]{:S(2)}) collective-permute-start(bf16[512,1024]{1,0:T(8,128)(2,1)} %slice.251), channel_id=1, source_target_pairs={{0,3},{1,4},{2,5},{3,6},{4,7},{5,8},{6,9},{7,10},{8,11},{9,12},{10... | collective-permute-start | bytes 3145736 | tf_op jit(solution)/shard_map/ppermute | solution.py:20
  207.4 68.2 %collective-permute-start.10 = (bf16[512,1024]{1,0:T(8,128)(2,1)}, bf16[512,1024]{1,0:T(8,128)(2,1)}, u32[]{:S(2)}, u32[]{:S(2)}) collective-permute-start(bf16[512,1024]{1,0:T(8,128)(2,1)} %slice.251), channel_id=1, source_target_pairs={{0,2},{1,3},{2,4},{3,5},{4,6},{5,7},{6,8},{7,9},{8,10},{9,11},{10,... | collective-permute-start | bytes 3145736 | tf_op jit(solution)/shard_map/ppermute | solution.py:20
  214.6 63.2 %collective-permute-start.11 = (bf16[512,1024]{1,0:T(8,128)(2,1)}, bf16[512,1024]{1,0:T(8,128)(2,1)S(1)}, u32[]{:S(2)}, u32[]{:S(2)}) collective-permute-start(bf16[512,1024]{1,0:T(8,128)(2,1)} %slice.251), channel_id=1, source_target_pairs={{0,1},{1,2},{2,3},{3,4},{4,5},{5,6},{6,7},{7,8},{8,9},{9,10},{10,1... | collective-permute-start | bytes 3145736 | tf_op jit(solution)/shard_map/ppermute | solution.py:20
  289.5 10.3 copy-start.15
  299.8 156.9 %copy-start.12 = (bf16[512,1024]{1,0:T(8,128)(2,1)S(1)}, bf16[512,1024]{1,0:T(8,128)(2,1)}, u32[]{:S(2)}) copy-start(bf16[512,1024]{1,0:T(8,128)(2,1)} %param.28) | copy-start | bytes 3145732
  302.6 2.3 copy-start
  312.3 2.3 copy-start
  351.2 2.3 copy-start
  390.4 2.3 copy-start
  400.1 2.3 copy-start
  409.8 2.3 copy-start
  419.5 2.3 copy-start
  456.7 4.7 copy-start.9
  461.4 858.9 %reduce-scatter.5.cloned.1.call-start = ((), (), s32[]{:S(2)}) async-start(), calls=%async_computation.8 | async-start | bytes 12976128 | tf_op jit(solution)/shard_map/reduce_scatter | solution.py:308
  662.6 10.3 copy-start.10
  662.6 16.0 slice-start
  662.6 16.0 slice-start.1
  662.6 16.0 slice-start.2
  672.9 29.3 %collective-permute-start.12 = (f32[512,1024]{0,1:T(8,128)}, f32[512,1024]{0,1:T(8,128)}, u32[]{:S(2)}, u32[]{:S(2)}) collective-permute-start(f32[512,1024]{0,1:T(8,128)} %bitcast.22), channel_id=1, source_target_pairs={{1,0},{2,1},{3,2},{4,3},{5,4},{6,5},{7,6},{8,7},{9,8},{10,9},{11,1... | collective-permute-start | bytes 6291464 | tf_op jit(solution)/shard_map/ppermute | solution.py:20
  674.3 115.9 %collective-permute-start.13 = (f32[512,1024]{0,1:T(8,128)}, f32[512,1024]{0,1:T(8,128)}, u32[]{:S(2)}, u32[]{:S(2)}) collective-permute-start(f32[512,1024]{0,1:T(8,128)} %bitcast.23), channel_id=1, source_target_pairs={{2,0},{3,1},{4,2},{5,3},{6,4},{7,5},{8,6},{9,7},{10,8},{11,9},{12,... | collective-permute-start | bytes 6291464 | tf_op jit(solution)/shard_map/ppermute | solution.py:20
  676.0 117.0 %collective-permute-start.14 = (f32[512,1024]{0,1:T(8,128)}, f32[512,1024]{0,1:T(8,128)}, u32[]{:S(2)}, u32[]{:S(2)}) collective-permute-start(f32[512,1024]{0,1:T(8,128)} %bitcast.24), channel_id=1, source_target_pairs={{3,0},{4,1},{5,2},{6,3},{7,4},{8,5},{9,6},{10,7},{11,8},{12,9},{13... | collective-permute-start | bytes 6291464 | tf_op jit(solution)/shard_map/ppermute | solution.py:20
  677.3 118.5 %collective-permute-start.15 = (f32[512,1024]{0,1:T(8,128)}, f32[512,1024]{0,1:T(8,128)}, u32[]{:S(2)}, u32[]{:S(2)}) collective-permute-start(f32[512,1024]{0,1:T(8,128)} %bitcast.25), channel_id=1, source_target_pairs={{4,0},{5,1},{6,2},{7,3},{8,4},{9,5},{10,6},{11,7},{12,8},{13,9},{1... | collective-permute-start | bytes 6291464 | tf_op jit(solution)/shard_map/ppermute | solution.py:20
  682.7 119.8 %collective-permute-start.16 = (f32[512,1024]{0,1:T(8,128)}, f32[512,1024]{0,1:T(8,128)S(1)}, u32[]{:S(2)}, u32[]{:S(2)}) collective-permute-start(f32[512,1024]{0,1:T(8,128)} %bitcast.206), channel_id=1, source_target_pairs={{1,0},{2,1},{3,2},{4,3},{5,4},{6,5},{7,6},{8,7},{9,8},{10,9},{11,1... | collective-permute-start | bytes 6291464 | tf_op jit(solution)/shard_map/ppermute | solution.py:20
  702.2 177.7 %collective-permute-start.17 = (f32[512,1024]{0,1:T(8,128)}, f32[512,1024]{0,1:T(8,128)S(1)}, u32[]{:S(2)}, u32[]{:S(2)}) collective-permute-start(f32[512,1024]{0,1:T(8,128)} %bitcast.205), channel_id=1, source_target_pairs={{2,0},{3,1},{4,2},{5,3},{6,4},{7,5},{8,6},{9,7},{10,8},{11,9},{12,... | collective-permute-start | bytes 6291464 | tf_op jit(solution)/shard_map/ppermute | solution.py:20
  790.2 91.2 %collective-permute-start.18 = (f32[512,1024]{0,1:T(8,128)}, f32[512,1024]{0,1:T(8,128)S(1)}, u32[]{:S(2)}, u32[]{:S(2)}) collective-permute-start(f32[512,1024]{0,1:T(8,128)} %bitcast.204), channel_id=1, source_target_pairs={{3,0},{4,1},{5,2},{6,3},{7,4},{8,5},{9,6},{10,7},{11,8},{12,9},{13... | collective-permute-start | bytes 6291464 | tf_op jit(solution)/shard_map/ppermute | solution.py:20
  793.0 88.4 %collective-permute-start.19 = (f32[512,1024]{0,1:T(8,128)}, f32[512,1024]{0,1:T(8,128)S(1)}, u32[]{:S(2)}, u32[]{:S(2)}) collective-permute-start(f32[512,1024]{0,1:T(8,128)} %bitcast.203), channel_id=1, source_target_pairs={{4,0},{5,1},{6,2},{7,3},{8,4},{9,5},{10,6},{11,7},{12,8},{13,9},{1... | collective-permute-start | bytes 6291464 | tf_op jit(solution)/shard_map/ppermute | solution.py:20
  795.8 5.7 copy-start.11
  795.8 5.7 copy-start.19
  802.4 80.3 %copy-start.3 = (bf16[512,16,64]{0,2,1:T(8,128)(2,1)}, bf16[512,16,64]{0,2,1:T(8,128)(2,1)S(1)}, u32[]{:S(2)}) copy-start(bf16[512,16,64]{0,2,1:T(8,128)(2,1)S(1)} %pad_maximum_fusion.1) | copy-start | bytes 3145732
  802.5 80.2 %copy-start.5 = (bf16[512,16,64]{0,2,1:T(8,128)(2,1)}, bf16[512,16,64]{0,2,1:T(8,128)(2,1)S(1)}, u32[]{:S(2)}) copy-start(bf16[512,16,64]{0,2,1:T(8,128)(2,1)S(1)} %pad_maximum_fusion.2) | copy-start | bytes 3145732
  881.4 2.3 copy-start.1
  881.4 2.3 copy-start.23
  881.4 2.3 copy-start.25
  881.4 2.3 copy-start.27
  881.4 2.3 copy-start.29
  893.4 586.2 %reduce-scatter.11.cloned.1.call-start = ((), (), s32[]{:S(2)}) async-start(), calls=%async_computation.11 | async-start | bytes 17301504 | tf_op jit(solution)/shard_map/reduce_scatter | solution.py:314
  1174.1 11.0 copy-start.13
  1233.5 433.5 %reduce-scatter.9.cloned.1.call-start = ((), (), s32[]{:S(2)}) async-start(), calls=%async_computation.10 | async-start | bytes 17301504 | tf_op jit(solution)/shard_map/reduce_scatter | solution.py:312
  1247.9 9.0 copy-start.8
  1256.9 7.7 copy-start.14
  1306.0 361.0 %copy-start.36 = (f32[32]{0:T(128)}, f32[32]{0:T(128)S(1)}, u32[]{:S(2)}) copy-start(f32[32]{0:T(128)S(1)} %dynamic-slice.11) | copy-start | bytes 388
  1309.5 8.5 copy-start.17
  1309.5 8.5 copy-start.35
  (19 other events, 29.5 us)
Sparse Core Ops, SparseCore 0:
  10.9 73.0 all-gather.5
  86.8 99.9 all-gather.7
  189.7 123.9 all-gather.9
  316.4 76.9 all-gather.11
  461.5 178.9 reduce-scatter.6
  893.5 401.1 reduce-scatter.4
  1297.6 181.8 reduce-scatter.10
  1482.5 184.4 reduce-scatter.8
where the time goes:
time: 1690 us; the launch traced here: 1670 us
  waiting for transfers between devices  645 us (38%)
  matrix products  408 us (24%)
  blocking collectives  360 us (21%)
  local copies, waits for them, and re-layouts  136 us (8%)
  other arithmetic  57.1 us (3%)
  starting transfers between devices  51.3 us (3%)
    all_gather x1, blocking collectives, on_device(): lax.all_gather(shards[5], 'fsdp', axis=0, tiled=True)  280 us
    ppermute x20, waiting for transfers between devices, shifted(): return lax.ppermute(block, axis, route)  219 us
    reduce_scatter x1, waiting for transfers between devices, on_device(): lax.psum_scatter(upper_weight_grad, 'fsdp', scatter_dimension=0, tiled=True)  187 us
    reduce_scatter x1, waiting for transfers between devices, on_device(): lax.psum_scatter(lower_weight_grad, 'fsdp', scatter_dimension=0, tiled=True)  159 us
    unnamed x2, blocking collectives  80.3 us
    all_gather x1, waiting for transfers between devices, on_device(): lax.all_gather(shards[2], 'fsdp', axis=0, tiled=True)  69.3 us
    dot_general x16, matrix products, head_forward(): jnp.dot(probabilities, values_in, preferred_element_type=jnp.float32)  61 us
    unnamed x115, local copies, waits for them, and re-layouts  56.8 us
  transfers between devices with their start and end apart: 28, of which 10 were waited for; matrix products, arithmetic and copies ran while one was open for 33% of the time, Pallas kernels for 0%

commit v1 on v0

v1 whole, which is shorter than its diff:
```python
from functools import partial

import jax
import jax.numpy as jnp
from jax import lax
from jax.experimental import pallas as pl
from jax.experimental.pallas import tpu as pltpu
from jax.sharding import PartitionSpec as P

HEAD_DIM = 64
ROT = 16
LMAX = 2048


norm_eps = 1e-05
masked_score = -1e30


def shifted(block, axis, distance):
    devices = range(lax.axis_size(axis))
    route = [(i - distance, i) for i in devices if i - distance in devices]
    return lax.ppermute(block, axis, route)


def layer_norm(values_in, gain_row, shift_row):
    mean_value = jnp.mean(values_in, axis=-1, keepdims=True)
    centred = values_in - mean_value
    variance = jnp.mean(centred * centred, axis=-1, keepdims=True)
    inverse = lax.rsqrt(variance + norm_eps)
    normal = centred * inverse
    return (normal * gain_row + shift_row, normal, inverse)


def norm_back(gradient, normal, inverse, gain_row):
    inner_sum = gradient * gain_row
    centred = inner_sum - jnp.mean(inner_sum, axis=-1, keepdims=True)
    return inverse * (centred - normal * jnp.mean(inner_sum * normal, axis=-1, keepdims=True))


def rotary_tables(positions):
    inverse = 10000.0 ** (-jnp.arange(0, ROT, 2, dtype=jnp.float32) / ROT)
    angles = positions.astype(jnp.float32)[:, None] * inverse[None, :]
    angles = jnp.concatenate([angles, angles], axis=-1)
    return (jnp.cos(angles), jnp.sin(angles))


def rotary_wide(positions, features):
    cos_table, sin_table = rotary_tables(positions)
    rows = positions.shape[0]
    middle = ROT // 2
    plain = HEAD_DIM - ROT
    none = jnp.zeros((rows, middle), jnp.float32)
    rest = jnp.zeros((rows, plain), jnp.float32)
    heads = features // HEAD_DIM
    stay = jnp.tile(jnp.concatenate([cos_table, rest + 1.0], axis=1), (1, heads))
    lower = jnp.tile(jnp.concatenate([sin_table[:, :middle], none, rest], axis=1), (1, heads))
    upper = jnp.tile(jnp.concatenate([none, sin_table[:, :middle], rest], axis=1), (1, heads))
    return (stay, lower, upper)


def rotate(rows, tables, sign):
    stay, lower, upper = tables
    middle = ROT // 2
    ahead = jnp.concatenate([rows[:, middle:], rows[:, :middle]], axis=1)
    behind = jnp.concatenate([rows[:, -middle:], rows[:, :-middle]], axis=1)
    return rows * stay + sign * (behind * upper - ahead * lower)


def owned_sum(parts, axis, order, send_type):
    devices = lax.axis_size(axis)
    place = lax.axis_index(axis)
    bits = devices.bit_length() - 1
    held = parts.reshape((2,) * bits + (parts.shape[0] // devices,) + parts.shape[1:])
    left = list(range(bits - 1, -1, -1))
    for bit in order:
        where = left.index(bit)
        mine = (place >> bit) & 1
        sent = lax.dynamic_index_in_dim(held, 1 - mine, where, keepdims=False)
        kept = lax.dynamic_index_in_dim(held, mine, where, keepdims=False)
        route = [(i, i ^ (1 << bit)) for i in range(devices)]
        got = lax.ppermute(sent.astype(send_type), axis, route)
        held = kept.astype(jnp.float32) + got.astype(jnp.float32)
        left.remove(bit)
    return held


def sum_order(devices, turn):
    bits = devices.bit_length() - 1
    middle = list(range(1, bits - 1))
    turn = turn % len(middle)
    return [0] + middle[turn:] + middle[:turn] + [bits - 1]


def heads_apart(rows):
    lane = lax.broadcasted_iota(jnp.int32, rows.shape, 1)
    zero = jnp.zeros_like(rows)
    return (
        jnp.where(lane < HEAD_DIM, rows, zero),
        jnp.where(lane < HEAD_DIM, zero, rows),
    )


def folded(tile, combine):
    return combine(tile.reshape(tile.shape[0] // 8, 8, tile.shape[1]), axis=0)


def attention_kernel(
    first_ref,
    query_segment_ref,
    key_segment_ref,
    query_ref,
    grad_ref,
    key_ref,
    value_ref,
    attended_ref,
    grad_query_ref,
    grad_pair_ref,
    bias_ref,
    weight_ref,
):
    rows = query_ref.shape[0]
    blocks = key_ref.shape[0] // rows
    first = first_ref[0]

    def span(block):
        return pl.ds(pl.multiple_of(block * rows, rows), rows)

    @pl.when(pl.program_id(0) == 0)
    def _():
        query_segment = query_segment_ref[...]
        column = lax.broadcasted_iota(jnp.int32, (rows, rows), 1)
        row = lax.broadcasted_iota(jnp.int32, (rows, rows), 0)
        for block in range(blocks):
            same = key_segment_ref[block * rows : (block + 1) * rows, :] == query_segment
            if block == blocks - 1:
                same = same & (row <= column)
            bias_ref[block * rows : (block + 1) * rows, :] = jnp.where(same, 0.0, masked_score)

    queries = heads_apart(query_ref[...])
    grads = heads_apart(grad_ref[...])
    across = (((1,), (1,)), ((), ()))

    def score_step(block, maxima):
        keys = key_ref[span(block), :]
        bias = bias_ref[span(block), :]
        found = []
        for head in range(2):
            scores = (
                lax.dot_general(keys, queries[head], across, preferred_element_type=jnp.float32)
                + bias
            )
            weight_ref[head, span(block), :] = scores
            found.append(jnp.maximum(maxima[head], folded(scores, jnp.max)))
        return tuple(found)

    start = jnp.full((8, rows), masked_score, jnp.float32)
    maxima = lax.fori_loop(first, blocks, score_step, (start, start))
    maxima = [jnp.max(entry, axis=0, keepdims=True) for entry in maxima]

    def value_step(block, carried):
        values_t = value_ref[span(block), :].T
        found = []
        for head in range(2):
            total, out = carried[head]
            exponent = jnp.exp(weight_ref[head, span(block), :] - maxima[head])
            weight_ref[head, span(block), :] = exponent
            total = total + folded(exponent, jnp.sum)
            out = out + jnp.dot(
                values_t[head * HEAD_DIM : (head + 1) * HEAD_DIM],
                exponent.astype(jnp.bfloat16),
                preferred_element_type=jnp.float32,
            )
            found.append((total, out))
        return tuple(found)

    zero_total = jnp.zeros((8, rows), jnp.float32)
    zero_out = jnp.zeros((HEAD_DIM, rows), jnp.float32)
    carried = lax.fori_loop(
        first, blocks, value_step, ((zero_total, zero_out), (zero_total, zero_out))
    )
    grads_t = grad_ref[...].astype(jnp.float32).T
    inverses, inners, outs = [], [], []
    for head in range(2):
        total, out = carried[head]
        inverse = 1.0 / jnp.sum(total, axis=0, keepdims=True)
        out = out * inverse
        inverses.append(inverse)
        outs.append(out)
        inners.append(
            jnp.sum(
                out * grads_t[head * HEAD_DIM : (head + 1) * HEAD_DIM], axis=0, keepdims=True
            )
        )
    attended_ref[...] = jnp.concatenate(outs, axis=0).T.astype(attended_ref.dtype)

    def clear_step(block, _):
        grad_pair_ref[block] = jnp.zeros(grad_pair_ref.shape[1:], grad_pair_ref.dtype)
        return 0

    lax.fori_loop(0, first, clear_step, 0)

    def back_step(block, carried):
        keys_t = key_ref[span(block), :].T
        values = value_ref[span(block), :]
        found = []
        grad_key = grad_value = None
        for head in range(2):
            probabilities = weight_ref[head, span(block), :] * inverses[head]
            grad_probs = lax.dot_general(
                values, grads[head], across, preferred_element_type=jnp.float32
            )
            grad_scores = (probabilities * (grad_probs - inners[head])).astype(jnp.bfloat16)
            key_part = jnp.dot(grad_scores, queries[head], preferred_element_type=jnp.float32)
            value_part = jnp.dot(
                probabilities.astype(jnp.bfloat16),
                grads[head],
                preferred_element_type=jnp.float32,
            )
            grad_key = key_part if head == 0 else grad_key + key_part
            grad_value = value_part if head == 0 else grad_value + value_part
            found.append(
                carried[head]
                + jnp.dot(
                    keys_t[head * HEAD_DIM : (head + 1) * HEAD_DIM],
                    grad_scores,
                    preferred_element_type=jnp.float32,
                )
            )
        grad_pair_ref[block, 0] = grad_key.astype(grad_pair_ref.dtype)
        grad_pair_ref[block, 1] = grad_value.astype(grad_pair_ref.dtype)
        return tuple(found)

    grad_queries = lax.fori_loop(first, blocks, back_step, (zero_out, zero_out))
    grad_query_ref[...] = jnp.concatenate(grad_queries, axis=0).T * HEAD_DIM ** (-0.5)


def attention(first, segment, ext_segment, queries, grads, ext_pairs):
    rows, features = queries.shape
    ext_rows = ext_pairs.shape[0]
    blocks = ext_rows // rows
    pair = 2 * HEAD_DIM
    short = pl.BlockSpec((rows, pair), lambda h, s: (0, h))
    pairs = features // pair
    keys = pl.BlockSpec((ext_rows, pair), lambda h, s: (0, h))
    values = pl.BlockSpec((ext_rows, pair), lambda h, s: (0, h + pairs))
    gradient = pl.BlockSpec((blocks, 2, rows, pair), lambda h, s: (0, 0, 0, h))
    scored = rows * ext_rows * features
    return pl.pallas_call(
        attention_kernel,
        out_shape=(
            jax.ShapeDtypeStruct((rows, features), jnp.bfloat16),
            jax.ShapeDtypeStruct((rows, features), jnp.float32),
            jax.ShapeDtypeStruct((blocks, 2, rows, features), jnp.bfloat16),
        ),
        grid_spec=pltpu.PrefetchScalarGridSpec(
            num_scalar_prefetch=1,
            grid=(pairs,),
            in_specs=[
                pl.BlockSpec((1, rows), lambda h, s: (0, 0)),
                pl.BlockSpec((ext_rows, 1), lambda h, s: (0, 0)),
                short,
                short,
                keys,
                values,
            ],
            out_specs=[short, short, gradient],
            scratch_shapes=[
                pltpu.VMEM((ext_rows, rows), jnp.float32),
                pltpu.VMEM((2, ext_rows, rows), jnp.float32),
            ],
        ),
        compiler_params=pltpu.CompilerParams(
            dimension_semantics=("arbitrary",), vmem_limit_bytes=44 * 1024 * 1024
        ),
        cost_estimate=pl.CostEstimate(
            flops=60 * scored, bytes_accessed=24 * ext_rows * features, transcendentals=0
        ),
    )(first, segment[None, :], ext_segment[:, None], queries, grads, ext_pairs, ext_pairs)


def on_device(
    hidden_in,
    cotangent,
    segment_ids,
    qkv_weight,
    qkv_bias,
    dense_weight,
    dense_bias,
    upper_weight,
    upper_bias,
    lower_weight,
    lower_bias,
    attn_norm_gain,
    attn_norm_bias,
    mlp_norm_gain,
    mlp_norm_bias,
):
    devices = lax.axis_size("fsdp")
    local_rows = hidden_in.shape[0]
    features = hidden_in.shape[1]
    share = dense_weight.shape[0]
    f32 = jnp.float32
    reach_devices = -(-LMAX // local_rows)
    offset = reach_devices * local_rows

    def gather(shard):
        return lax.all_gather(shard, "fsdp", axis=0, tiled=True)

    vectors = (
        qkv_bias,
        dense_bias,
        upper_bias,
        lower_bias,
        attn_norm_gain,
        attn_norm_bias,
        mlp_norm_gain,
        mlp_norm_bias,
    )
    columns = jnp.concatenate([entry.reshape(share, -1) for entry in vectors], axis=1)
    columns = jnp.pad(columns, ((0, 0), (0, 128 - columns.shape[1])))
    dense_wide = gather(jnp.concatenate([dense_weight, columns], axis=1))
    dense_full = dense_wide[:, :features]
    rows_out = []
    at = features
    for entry in vectors:
        width = entry.shape[0] // share
        rows_out.append(dense_wide[:, at : at + width].reshape(-1).astype(f32))
        at += width
    qkv_row, dense_row, upper_row, lower_row, gain_attn, shift_attn, gain_mlp, shift_mlp = rows_out
    qkv_full = gather(qkv_weight)
    upper_full = gather(upper_weight)
    lower_full = gather(lower_weight)

    segment_plus = segment_ids + 1
    earlier = [shifted(segment_plus, "fsdp", distance) for distance in range(reach_devices, 0, -1)]
    ext_segment = jnp.concatenate(earlier + [segment_plus])
    below_count = jnp.sum((ext_segment[None, :] < segment_plus[:, None]).astype(jnp.int32), axis=1)
    positions = jnp.arange(local_rows, dtype=jnp.int32) + offset - below_count
    lasts = jnp.stack([entry[-1] for entry in earlier])
    first = jnp.sum((lasts != segment_plus[0]).astype(jnp.int32)).reshape(1)
    tables = rotary_wide(positions, features)

    hidden_f = hidden_in.astype(f32)
    normed_attn, normal_attn, inverse_attn = layer_norm(hidden_f, gain_attn, shift_attn)
    normed_attn = normed_attn.astype(jnp.bfloat16)
    projected = jnp.dot(normed_attn, qkv_full, preferred_element_type=f32) + qkv_row
    query_rot = rotate(projected[:, :features], tables, 1.0) * HEAD_DIM ** (-0.5)
    query_rot = query_rot.astype(jnp.bfloat16)
    key_rot = rotate(projected[:, features : 2 * features], tables, 1.0).astype(jnp.bfloat16)
    value_low = projected[:, 2 * features :].astype(jnp.bfloat16)
    own_pair = jnp.concatenate([key_rot, value_low], axis=1)
    fetched = [shifted(own_pair, "fsdp", distance) for distance in range(reach_devices, 0, -1)]
    ext_pairs = jnp.concatenate(fetched + [own_pair])
    grad_attended = jnp.einsum("te,de->td", cotangent, dense_full, preferred_element_type=f32)
    grad_attended = grad_attended.astype(jnp.bfloat16)

    attended, grad_query, grad_pairs = attention(
        first, segment_plus, ext_segment, query_rot, grad_attended, ext_pairs
    )
    returned = [
        shifted(grad_pairs[reach_devices - distance], "fsdp", -distance)
        for distance in range(1, reach_devices + 1)
    ]

    normed_mlp, normal_mlp, inverse_mlp = layer_norm(hidden_f, gain_mlp, shift_mlp)
    normed_mlp = normed_mlp.astype(jnp.bfloat16)
    upper = jnp.dot(normed_mlp, upper_full, preferred_element_type=f32) + upper_row
    gelu_exact = partial(jax.nn.gelu, approximate=False)
    active, gelu_pull = jax.vjp(gelu_exact, upper)
    active = active.astype(jnp.bfloat16)
    low = jnp.bfloat16
    cotangent_f = cotangent.astype(f32)

    def weight_grad(left, right, turn):
        product = lax.dot_general(
            left, right, (((0,), (0,)), ((), ())), preferred_element_type=f32
        ).astype(low)
        order = sum_order(devices, turn)
        return owned_sum(product, "fsdp", order, low)

    lower_weight_grad = weight_grad(active, cotangent, 0)
    grad_active = jnp.einsum("td,fd->tf", cotangent, lower_full, preferred_element_type=f32)
    grad_upper = gelu_pull(grad_active)[0].astype(low)
    upper_weight_grad = weight_grad(normed_mlp, grad_upper, 1)
    dense_weight_grad = weight_grad(attended, cotangent, 2)
    mlp_branch = jnp.dot(active, lower_full, preferred_element_type=f32) + lower_row
    attn_branch = jnp.dot(attended, dense_full, preferred_element_type=f32) + dense_row
    hidden_out = (hidden_f + attn_branch + mlp_branch).astype(jnp.bfloat16)
    column_sums = jnp.sum(cotangent_f, axis=0)
    upper_bias_grad = jnp.sum(grad_upper.astype(f32), axis=0)
    grad_norm_mlp = jnp.einsum("tf,df->td", grad_upper, upper_full, preferred_element_type=f32)
    mlp_gain_grad = jnp.sum(grad_norm_mlp * normal_mlp, axis=0)
    mlp_shift_grad = jnp.sum(grad_norm_mlp, axis=0)

    own_grad = grad_pairs[reach_devices].astype(f32)
    for entry in returned:
        own_grad = own_grad + entry.astype(f32)
    grad_query = rotate(grad_query, tables, -1.0).astype(low)
    grad_key = rotate(own_grad[0], tables, -1.0).astype(low)
    grad_value = own_grad[1].astype(low)
    grad_qkv = jnp.concatenate([grad_query, grad_key, grad_value], axis=1)
    qkv_weight_grad = jnp.concatenate(
        [
            weight_grad(normed_attn, grad_query, 0),
            weight_grad(normed_attn, grad_key, 1),
            weight_grad(normed_attn, grad_value, 2),
        ],
        axis=1,
    )
    qkv_bias_grad = jnp.sum(grad_qkv.astype(f32), axis=0)
    grad_norm_attn = jnp.einsum("tj,dj->td", grad_qkv, qkv_full, preferred_element_type=f32)
    attn_gain_grad = jnp.sum(grad_norm_attn * normal_attn, axis=0)
    attn_shift_grad = jnp.sum(grad_norm_attn, axis=0)
    hidden_grad = (
        cotangent_f
        + norm_back(grad_norm_attn, normal_attn, inverse_attn, gain_attn)
        + norm_back(grad_norm_mlp, normal_mlp, inverse_mlp, gain_mlp)
    )
    sums = (
        qkv_bias_grad,
        column_sums,
        upper_bias_grad,
        attn_gain_grad,
        attn_shift_grad,
        mlp_gain_grad,
        mlp_shift_grad,
    )
    packed = jnp.concatenate([entry.reshape(devices, -1) for entry in sums], axis=1)
    packed = owned_sum(packed, "fsdp", sum_order(devices, 0), f32).reshape(-1)
    pieces = []
    at = 0
    for entry in sums:
        width = entry.shape[0] // devices
        pieces.append(packed[at : at + width])
        at += width
    return (
        hidden_out,
        hidden_grad,
        qkv_weight_grad,
        pieces[0],
        dense_weight_grad,
        pieces[1],
        upper_weight_grad,
        pieces[2],
        lower_weight_grad,
        pieces[1],
        pieces[3],
        pieces[4],
        pieces[5],
        pieces[6],
    )


def solution(mesh):
    placed = (
        P("fsdp", None),
        P("fsdp", None),
        P("fsdp"),
        P("fsdp", None),
        P("fsdp"),
        P("fsdp", None),
        P("fsdp"),
        P("fsdp", None),
        P("fsdp"),
        P("fsdp", None),
        P("fsdp"),
        P("fsdp"),
        P("fsdp"),
        P("fsdp"),
        P("fsdp"),
    )
    return jax.shard_map(
        on_device,
        mesh=mesh,
        in_specs=placed,
        out_specs=(
            P("fsdp", None),
            P("fsdp", None),
            P("fsdp", None),
            P("fsdp"),
            P("fsdp", None),
            P("fsdp"),
            P("fsdp", None),
            P("fsdp"),
            P("fsdp", None),
            P("fsdp"),
            P("fsdp"),
            P("fsdp"),
            P("fsdp"),
            P("fsdp"),
        ),
        check_vma=False,
    )
```

time: 1690 us -> 811 us (0.48)
  blocking collectives: 360 us -> 0 us
  matrix products: 408 us -> 95.6 us
  waiting for transfers between devices: 645 us -> 357 us
  starting transfers between devices: 51.3 us -> 164 us
  local copies, waits for them, and re-layouts: 136 us -> 84.2 us
  Pallas kernels: 0 us -> 26.6 us
    reduce_scatter x4 -> x0, waiting for transfers between devices: 347 us -> none  [the longest x1 187 us: on_device(): lax.psum_scatter(upper_weight_grad, 'fsdp', scatter_dimension=0, tiled=True)]
    dot_general x124 -> x14, matrix products: 408 us -> 95.6 us  [the longest x1 27.9 us: on_device(): jnp.einsum('td,fd->tf', cotangent, lower_full, preferred_element_type=f32)]
    all_gather x1 -> x0, blocking collectives: 280 us -> none  [on_device(): lax.all_gather(shards[5], 'fsdp', axis=0, tiled=True)]
    ppermute x0 -> x35, starting transfers between devices: none -> 129 us  [owned_sum(): got = lax.ppermute(sent.astype(send_type), axis, route)]
    ppermute x0 -> x35, waiting for transfers between devices: none -> 97.6 us  [owned_sum(): got = lax.ppermute(sent.astype(send_type), axis, route)]
    ppermute x20 -> x12, waiting for transfers between devices: 219 us -> 131 us  [shifted(): return lax.ppermute(block, axis, route)]
    unnamed x2 -> x0, blocking collectives: 80.3 us -> none
    all_gather x4, waiting for transfers between devices: 77.4 us -> 127 us  [gather(): return lax.all_gather(shard, 'fsdp', axis=0, tiled=True)]
  transfers between devices with their start and end apart: 28 -> 51, of which waited for: 10 -> 22; matrix products, arithmetic and copies ran while one was open for 33% -> 28% of each run, Pallas kernels for 0% -> 3%
where the time goes in v1:
time: 811 us; the launch traced here: 804 us
  waiting for transfers between devices  357 us (44%)
  starting transfers between devices  164 us (20%)
  matrix products  95.6 us (12%)
  local copies, waits for them, and re-layouts  84.2 us (10%)
  other arithmetic  61.1 us (8%)
  Pallas kernels  26.6 us (3%)
  between operations  15.5 us (2%)
    ppermute x12, waiting for transfers between devices, shifted(): return lax.ppermute(block, axis, route)  131 us
    ppermute x35, starting transfers between devices, owned_sum(): got = lax.ppermute(sent.astype(send_type), axis, route)  129 us
    all_gather x4, waiting for transfers between devices, gather(): return lax.all_gather(shard, 'fsdp', axis=0, tiled=True)  127 us
    ppermute x35, waiting for transfers between devices, owned_sum(): got = lax.ppermute(sent.astype(send_type), axis, route)  97.6 us
    ppermute x12, starting transfers between devices, shifted(): return lax.ppermute(block, axis, route)  35.5 us
    dot_general x1, matrix products, on_device(): jnp.einsum('td,fd->tf', cotangent, lower_full, preferred_element_type=f32)  27.9 us
    pallas_call x1, Pallas kernels, attention(): pl.pallas_call(attention_kernel, out_shape=(jax.ShapeDtypeStruct((rows, f...  26.6 us
    dot_general x6, matrix products, weight_grad(): lax.dot_general(left, right, (((0,), (0,)), ((), ())), preferred_element_...  24.8 us
  transfers between devices with their start and end apart: 51, of which 22 were waited for; matrix products, arithmetic and copies ran while one was open for 28% of the time, Pallas kernels for 3%

profile of v1, /device:TPU:0, one launch (start us, length us, event | category | flops | bytes accessed | tf_op | source)
XLA Modules:
  0.0 804.2 jit_solution(9484104104817642316)
XLA Ops:
  17.2 2.3 collective-permute-start.3
  19.6 4.4 collective-permute-start.2
  24.0 4.3 collective-permute-start.1
  28.3 3.4 collective-permute-start
  40.2 2.9 copy.87
  44.7 3.0 copy.88
  47.7 27.4 %all-gather.5.cloned.1.call-done = bf16[1024,1152]{1,0:T(8,128)(2,1)} async-done(((bf16[32,1152]{1,0:T(8,128)(2,1)}), bf16[1024,1152]{1,0:T(8,128)(2,1)}) %all-gather.5.cloned.1.call-update) | async-done | bytes 2359312 | tf_op jit(solution)/shard_map/all_gather | solution.py:307
  78.2 3.5 convert_reduce_fusion.10
  81.7 64.7 %all-gather.7.cloned.1.call-done = bf16[1024,3072]{1,0:T(8,128)(2,1)} async-done(((bf16[32,3072]{1,0:T(8,128)(2,1)}), bf16[1024,3072]{1,0:T(8,128)(2,1)}) %all-gather.7.cloned.1.call-update) | async-done | bytes 6291472 | tf_op jit(solution)/shard_map/all_gather | solution.py:307
  146.4 5.8 convolution_add_fusion
  153.6 2.8 fusion.115
  156.4 4.1 fusion.38
  162.2 4.7 collective-permute-start.4
  166.9 3.4 collective-permute-start.5
  170.3 4.3 collective-permute-start.6
  174.6 2.9 collective-permute-start.7
  180.8 3.9 fusion.105
  186.1 3.1 fusion.59.grad_ref
  189.3 131.1 %collective-permute-done.4 = bf16[512,2048]{1,0:T(8,128)(2,1)} collective-permute-done((bf16[512,2048]{1,0:T(8,128)(2,1)}, bf16[512,2048]{1,0:T(8,128)(2,1)}, u32[]{:S(2)}, u32[]{:S(2)}) %collective-permute-start.4) | collective-permute-done | bytes 2097184 | tf_op jit(solution)/shard_map/ppermute | solution.py:22
  328.5 3.9 copy-done.29
  332.4 26.6 %shard_map.254 = (bf16[512,1024]{1,0:T(8,128)(2,1)S(1)}, f32[512,1024]{1,0:T(8,128)S(1)}, bf16[5,2,512,1024]{3,2,1,0:T(8,128)(2,1)}) custom-call(s32[1]{0:T(128)} %bitcast.1.first_ref, s32[1,512]{1,0:T(1,128)S(1)} %bitcast.243, s32[2560,1]{1,0:T(8,128)S(1)} %broadcast_in_dim.12.key_segment_ref, bf16[512,1024]{1,0:T(8,128)(2,1)S(1)} %get-tuple-element.42.query_ref, ...), custom_call_target="tpu_custom_call" | custom-call | flops 80530636800 | bytes 62914560 | tf_op jit(solution)/shard_map/pallas_call | solution.py:248
  359.0 6.8 slice_bitcast_fusion.4
  372.4 2.7 convolution_convert_fusion.2
  375.1 2.9 fusion.117
  378.0 10.3 %fusion.108 = f32[512,4096]{1,0:T(8,128)} fusion(bf16[1024,4096]{1,0:T(8,128)(2,1)} %all-gather.9.cloned.1.call-done, bf16[512,1024]{1,0:T(8,128)(2,1)S(1)} %copy-done.12, f32[1024]{0:T(1024)S(1)} %get-tuple-element.26, f32[1024]{0:T(1024)S(1)} %get-tuple-element.27, f32[512]{0:T(512)S(1)} %add_rsqrt_fusion, f32[512]{0:T(512)S(1)} %broadcast_multiply_fusion.5), kind=kOutput, calls=%fused_computation.280 | convolution fusion | flops 4298113024 | bytes 17838080 | tf_op jit(solution)/shard_map/dot_general | solution.py:367
  388.3 34.8 %all-gather.11.cloned.1.call-done = bf16[4096,1024]{1,0:T(8,128)(2,1)} async-done(((bf16[128,1024]{1,0:T(8,128)(2,1)}), bf16[4096,1024]{1,0:T(8,128)(2,1)}) %all-gather.11.cloned.1.call-update) | async-done | bytes 8388624 | tf_op jit(solution)/shard_map/all_gather | solution.py:307
  423.1 27.9 %convert_reduce_fusion = (f32[4096]{0:T(1024)S(1)}, bf16[512,4096]{1,0:T(8,128)(2,1)}, f32[512,4096]{1,0:T(8,128)}) fusion(f32[512,4096]{1,0:T(8,128)} %fusion.108, f32[4096]{0:T(1024)S(1)} %reshape.284, bf16[512,1024]{1,0:T(8,128)(2,1)S(1)} %copy-done.27, bf16[4096,1024]{1,0:T(8,128)(2,1)} %all-gather.11.cloned.1.call-done), kind=kOutput, calls=%fused_computation.4 | convolution fusion | flops 4452249600 | bytes 30441472 | tf_op jit(solution)/shard_map/td,fd->tf/dot_general | solution.py:382
  451.0 9.8 %multiply_convert_fusion = bf16[512,4096]{1,0:T(8,128)(2,1)} fusion(f32[512,4096]{1,0:T(8,128)} %get-tuple-element.40, f32[512,4096]{1,0:T(8,128)} %fusion.108, f32[4096]{0:T(1024)S(1)} %reshape.284), kind=kLoop, calls=%fused_computation.6 | loop fusion | flops 8388608 | bytes 20987904 | tf_op jit(solution)/shard_map/convert_element_type | solution.py:370
  460.8 9.4 %convolution_convert_fusion.1 = bf16[1024,4096]{1,0:T(8,128)(2,1)} fusion(bf16[512,4096]{1,0:T(8,128)(2,1)} %get-tuple-element.39, bf16[512,1024]{1,0:T(8,128)(2,1)S(1)} %copy-done.12, f32[1024]{0:T(1024)S(1)} %get-tuple-element.26, f32[1024]{0:T(1024)S(1)} %get-tuple-element.27, f32[512]{0:T(512)S(1)} %add_rsqrt_fusion, f32[512]{0:T(512)S(1)} %broadcast_multiply_fusion.5), kind=kOutput, calls=%fused_computation.21 | convolution fusion | flops 4302307328 | bytes 13643776 | tf_op jit(solution)/shard_map/dot_general | solution.py:375
  470.2 6.3 constant_dynamic-slice_fusion.3
  476.5 2.4 copy.144
  478.9 5.2 collective-permute-start.37
  484.1 6.8 convolution_convert_fusion
  490.9 7.0 constant_dynamic-slice_fusion.1
  497.8 2.8 copy.143
  500.6 7.2 fusion.122
  507.9 2.4 fusion.34
  510.3 5.9 fusion.123
  517.4 6.5 fusion.8
  530.3 2.6 fusion.47
  534.6 8.2 %fusion.30 = (f32[1024]{0:T(1024)S(1)}, f32[512]{0:T(512)S(1)}, f32[512]{0:T(512)S(1)}, f32[1024]{0:T(1024)S(1)}, f32[1024]{0:T(1024)S(1)}, /*index=5*/f32[512]{...) fusion(bf16[512,1024]{1,0:T(8,128)(2,1)S(1)} %copy-done.12, f32[512]{0:T(512)S(1)} %add_rsqrt_fusion, ...), kind=kOutput, calls=%fused_computation.64 | convolution fusion | flops 3239569408 | bytes 14716928 | tf_op jit(solution)/shard_map/tj,dj->td/dot_general | solution.py:411
  542.8 2.9 convert_reduce_fusion.4
  546.5 3.1 convolution_convert_fusion.3
  549.7 41.2 %collective-permute-start.28 = (f32[2,2,2,1,384]{4,3,2,1,0:T(1,128)S(1)}, f32[2,2,2,1,384]{4,3,2,1,0:T(1,128)S(1)}, u32[]{:S(2)}, u32[]{:S(2)}) collective-permute-start(f32[2,2,2,1,384]{4,3,2,1,0:T(1,128)S(1)} %fusion.95), channel_id=1, source_target_pairs={{0,2},{1,3},{2,0},{3,1},{4,6},{5,7},{6,4},{7,5},{8,10},{9,11},{10,... | collective-permute-start | bytes 36872 | tf_op jit(solution)/shard_map/ppermute | solution.py:81
  592.7 28.2 %collective-permute-start.29 = (f32[2,2,1,384]{3,2,1,0:T(1,128)S(1)}, f32[2,2,1,384]{3,2,1,0:T(1,128)S(1)}, u32[]{:S(2)}, u32[]{:S(2)}) collective-permute-start(f32[2,2,1,384]{3,2,1,0:T(1,128)S(1)} %fusion.98), channel_id=1, source_target_pairs={{0,4},{1,5},{2,6},{3,7},{4,0},{5,1},{6,2},{7,3},{8,12},{9,13},{10,... | collective-permute-start | bytes 18440 | tf_op jit(solution)/shard_map/ppermute | solution.py:81
  622.5 6.0 collective-permute-start.30
  630.2 11.2 %collective-permute-start.31 = (f32[1,384]{1,0:T(1,128)S(1)}, f32[1,384]{1,0:T(1,128)S(1)}, u32[]{:S(2)}, u32[]{:S(2)}) collective-permute-start(f32[1,384]{1,0:T(1,128)S(1)} %fusion.104), channel_id=1, source_target_pairs={{0,16},{1,17},{2,18},{3,19},{4,20},{5,21},{6,22},{7,23},{8,24},{9,... | collective-permute-start | bytes 4616 | tf_op jit(solution)/shard_map/ppermute | solution.py:81
  649.1 2.1 collective-permute-start.13
  651.7 8.0 %collective-permute-done.23 = bf16[2,2,2,32,1024]{4,3,0,1,2:T(8,128)(2,1)S(1)} collective-permute-done((bf16[2,2,2,32,1024]{4,3,0,1,2:T(8,128)(2,1)S(1)}, bf16[2,2,2,32,1024]{4,3,0,1,2:T(8,128)(2,1)S(1)}, u32[]{:S(2)}, u32[]{:S(2)}) %collective-permute-start.23) | collective-permute-done | bytes 524320 | tf_op jit(solution)/shard_map/ppermute | solution.py:81
  664.8 9.8 %collective-permute-done.33 = bf16[2,2,2,32,1024]{4,3,0,1,2:T(8,128)(2,1)S(1)} collective-permute-done((bf16[2,2,2,32,1024]{4,3,0,1,2:T(8,128)(2,1)S(1)}, bf16[2,2,2,32,1024]{4,3,0,1,2:T(8,128)(2,1)S(1)}, u32[]{:S(2)}, u32[]{:S(2)}) %collective-permute-start.33) | collective-permute-done | bytes 524320 | tf_op jit(solution)/shard_map/ppermute | solution.py:81
  686.7 2.9 collective-permute-start.26
  689.6 3.7 convert_add_fusion.1
  695.6 2.9 collective-permute-start.16
  700.5 4.2 convert_add_fusion
  705.0 2.3 collective-permute-start.43
  707.3 32.3 %collective-permute-done.38 = bf16[2,2,2,32,4096]{4,3,0,2,1:T(8,128)(2,1)} collective-permute-done((bf16[2,2,2,32,4096]{4,3,0,2,1:T(8,128)(2,1)}, bf16[2,2,2,32,4096]{4,3,0,2,1:T(8,128)(2,1)}, u32[]{:S(2)}, u32[]{:S(2)}) %collective-permute-start.38) | collective-permute-done | bytes 2097184 | tf_op jit(solution)/shard_map/ppermute | solution.py:81
  739.6 2.3 bitcast_add_fusion.1
  743.7 6.0 collective-permute-done.43
  752.3 10.7 %collective-permute-done.39 = bf16[2,2,32,4096]{3,2,0,1:T(8,128)(2,1)S(1)} collective-permute-done((bf16[2,2,32,4096]{3,2,0,1:T(8,128)(2,1)S(1)}, bf16[2,2,32,4096]{3,2,0,1:T(8,128)(2,1)S(1)}, u32[]{:S(2)}, u32[]{:S(2)}) %collective-permute-start.39) | collective-permute-done | bytes 1048608 | tf_op jit(solution)/shard_map/ppermute | solution.py:81
  763.3 3.1 collective-permute-start.40
  767.0 4.7 collective-permute-done.44
  772.2 2.1 collective-permute-done.40
  776.2 10.1 %collective-permute-done.45 = bf16[2,128,1024]{2,1,0:T(8,128)(2,1)S(1)} collective-permute-done((bf16[2,128,1024]{2,1,0:T(8,128)(2,1)S(1)}, bf16[2,128,1024]{2,1,0:T(8,128)(2,1)S(1)}, u32[]{:S(2)}, u32[]{:S(2)}) %collective-permute-start.45) | collective-permute-done | bytes 524320 | tf_op jit(solution)/shard_map/ppermute | solution.py:81
  788.7 7.5 collective-permute-done.46
  (300 shorter events, 101.0 us)
Async XLA Ops:
  7.2 26.6 %copy-start.32 = (s32[512]{0:T(512)S(1)}, s32[512]{0:T(512)}, u32[]{:S(2)}) copy-start(s32[512]{0:T(512)} %param.17) | copy-start | bytes 6148
  7.2 26.0 %copy-start.11 = (bf16[512,1024]{1,0:T(8,128)(2,1)S(1)}, bf16[512,1024]{1,0:T(8,128)(2,1)}, u32[]{:S(2)}) copy-start(bf16[512,1024]{1,0:T(8,128)(2,1)} %param.15) | copy-start | bytes 3145732
  7.2 67.9 %all-gather.5.cloned.1.call-start = ((), (), s32[]{:S(2)}) async-start(), calls=%async_computation | async-start | bytes 2433024 | tf_op jit(solution)/shard_map/all_gather | solution.py:307
  15.0 131.4 %all-gather.7.cloned.1.call-start = ((), (), s32[]{:S(2)}) async-start(), calls=%async_computation.1 | async-start | bytes 6488064 | tf_op jit(solution)/shard_map/all_gather | solution.py:307
  15.7 362.2 %all-gather.9.cloned.1.call-start = ((), (), s32[]{:S(2)}) async-start(), calls=%async_computation.2 | async-start | bytes 8650752 | tf_op jit(solution)/shard_map/all_gather | solution.py:307
  16.5 406.6 %all-gather.11.cloned.1.call-start = ((), (), s32[]{:S(2)}) async-start(), calls=%async_computation.3 | async-start | bytes 8650752 | tf_op jit(solution)/shard_map/all_gather | solution.py:307
  17.2 16.6 %collective-permute-start.3 = (s32[512]{0:T(512)S(1)}, s32[512]{0:T(512)S(1)}, u32[]{:S(2)}, u32[]{:S(2)}) collective-permute-start(s32[512]{0:T(512)S(1)} %broadcast_add_fusion), channel_id=1, source_target_pairs={{0,1},{1,2},{2,3},{3,4},{4,5},{5,6},{6,7},{7,8},{8,9},{9,10},{10,1... | collective-permute-start | bytes 6152 | tf_op jit(solution)/shard_map/ppermute | solution.py:22
  19.6 14.2 %collective-permute-start.2 = (s32[512]{0:T(512)S(1)}, s32[512]{0:T(512)S(1)}, u32[]{:S(2)}, u32[]{:S(2)}) collective-permute-start(s32[512]{0:T(512)S(1)} %broadcast_add_fusion), channel_id=1, source_target_pairs={{0,2},{1,3},{2,4},{3,5},{4,6},{5,7},{6,8},{7,9},{8,10},{9,11},{10,... | collective-permute-start | bytes 6152 | tf_op jit(solution)/shard_map/ppermute | solution.py:22
  24.0 9.8 %collective-permute-start.1 = (s32[512]{0:T(512)S(1)}, s32[512]{0:T(512)S(1)}, u32[]{:S(2)}, u32[]{:S(2)}) collective-permute-start(s32[512]{0:T(512)S(1)} %broadcast_add_fusion), channel_id=1, source_target_pairs={{0,3},{1,4},{2,5},{3,6},{4,7},{5,8},{6,9},{7,10},{8,11},{9,12},{10... | collective-permute-start | bytes 6152 | tf_op jit(solution)/shard_map/ppermute | solution.py:22
  28.3 5.4 collective-permute-start
  38.3 118.1 %copy-start.3 = (f32[512,1024]{1,0:T(8,128)}, f32[512,1024]{1,0:T(8,128)S(1)}, u32[]{:S(2)}) copy-start(f32[512,1024]{1,0:T(8,128)S(1)} %copy.86) | copy-start | bytes 6291460
  81.7 70.5 %copy-start.30 = (f32[1024]{0:T(1024)}, f32[1024]{0:T(1024)S(1)}, u32[]{:S(2)}) copy-start(f32[1024]{0:T(1024)S(1)} %get-tuple-element.24) | copy-start | bytes 12292
  81.7 70.5 %copy-start.33 = (f32[1024]{0:T(1024)}, f32[1024]{0:T(1024)S(1)}, u32[]{:S(2)}) copy-start(f32[1024]{0:T(1024)S(1)} %get-tuple-element.29) | copy-start | bytes 12292
  162.2 158.2 %collective-permute-start.4 = (bf16[512,2048]{1,0:T(8,128)(2,1)}, bf16[512,2048]{1,0:T(8,128)(2,1)}, u32[]{:S(2)}, u32[]{:S(2)}) collective-permute-start(bf16[512,2048]{1,0:T(8,128)(2,1)} %pad_maximum_fusion.1), channel_id=1, source_target_pairs={{0,4},{1,5},{2,6},{3,7},{4,8},{5,9},{6,10},{7,11},{8,12},{9,13},{1... | collective-permute-start | bytes 6291464 | tf_op jit(solution)/shard_map/ppermute | solution.py:22
  166.9 155.5 %collective-permute-start.5 = (bf16[512,2048]{1,0:T(8,128)(2,1)}, bf16[512,2048]{1,0:T(8,128)(2,1)}, u32[]{:S(2)}, u32[]{:S(2)}) collective-permute-start(bf16[512,2048]{1,0:T(8,128)(2,1)} %pad_maximum_fusion.1), channel_id=1, source_target_pairs={{0,3},{1,4},{2,5},{3,6},{4,7},{5,8},{6,9},{7,10},{8,11},{9,12},{10... | collective-permute-start | bytes 6291464 | tf_op jit(solution)/shard_map/ppermute | solution.py:22
  170.3 154.0 %collective-permute-start.6 = (bf16[512,2048]{1,0:T(8,128)(2,1)}, bf16[512,2048]{1,0:T(8,128)(2,1)}, u32[]{:S(2)}, u32[]{:S(2)}) collective-permute-start(bf16[512,2048]{1,0:T(8,128)(2,1)} %pad_maximum_fusion.1), channel_id=1, source_target_pairs={{0,2},{1,3},{2,4},{3,5},{4,6},{5,7},{6,8},{7,9},{8,10},{9,11},{10,... | collective-permute-start | bytes 6291464 | tf_op jit(solution)/shard_map/ppermute | solution.py:22
  174.6 151.6 %collective-permute-start.7 = (bf16[512,2048]{1,0:T(8,128)(2,1)}, bf16[512,2048]{1,0:T(8,128)(2,1)}, u32[]{:S(2)}, u32[]{:S(2)}) collective-permute-start(bf16[512,2048]{1,0:T(8,128)(2,1)} %pad_maximum_fusion.1), channel_id=1, source_target_pairs={{0,1},{1,2},{2,3},{3,4},{4,5},{5,6},{6,7},{7,8},{8,9},{9,10},{10,1... | collective-permute-start | bytes 6291464 | tf_op jit(solution)/shard_map/ppermute | solution.py:22
  359.0 16.1 %copy-start = (f32[512,1024]{1,0:T(8,128)}, f32[512,1024]{1,0:T(8,128)S(1)}, u32[]{:S(2)}) copy-start(f32[512,1024]{1,0:T(8,128)S(1)} %get-tuple-element.18) | copy-start | bytes 6291460
  359.0 13.4 %copy-start.27 = (bf16[512,1024]{1,0:T(8,128)(2,1)S(1)}, bf16[512,1024]{1,0:T(8,128)(2,1)}, u32[]{:S(2)}) copy-start(bf16[512,1024]{1,0:T(8,128)(2,1)} %param.16) | copy-start | bytes 3145732
  365.8 150.3 %collective-permute-start.11 = (bf16[2,512,1024]{2,1,0:T(8,128)(2,1)}, bf16[2,512,1024]{2,1,0:T(8,128)(2,1)}, u32[]{:S(2)}, u32[]{:S(2)}) collective-permute-start(bf16[2,512,1024]{2,1,0:T(8,128)(2,1)} %get-tuple-element.44), channel_id=1, source_target_pairs={{4,0},{5,1},{6,2},{7,3},{8,4},{9,5},{10,6},{11,7},{12,8},{13,9},{1... | collective-permute-start | bytes 6291464 | tf_op jit(solution)/shard_map/ppermute | solution.py:22
  367.1 150.3 %collective-permute-start.10 = (bf16[2,512,1024]{2,1,0:T(8,128)(2,1)}, bf16[2,512,1024]{2,1,0:T(8,128)(2,1)}, u32[]{:S(2)}, u32[]{:S(2)}) collective-permute-start(bf16[2,512,1024]{2,1,0:T(8,128)(2,1)} %get-tuple-element.45), channel_id=1, source_target_pairs={{3,0},{4,1},{5,2},{6,3},{7,4},{8,5},{9,6},{10,7},{11,8},{12,9},{13... | collective-permute-start | bytes 6291464 | tf_op jit(solution)/shard_map/ppermute | solution.py:22
  368.4 149.0 %collective-permute-start.9 = (bf16[2,512,1024]{2,1,0:T(8,128)(2,1)}, bf16[2,512,1024]{2,1,0:T(8,128)(2,1)}, u32[]{:S(2)}, u32[]{:S(2)}) collective-permute-start(bf16[2,512,1024]{2,1,0:T(8,128)(2,1)} %get-tuple-element.46), channel_id=1, source_target_pairs={{2,0},{3,1},{4,2},{5,3},{6,4},{7,5},{8,6},{9,7},{10,8},{11,9},{12,... | collective-permute-start | bytes 6291464 | tf_op jit(solution)/shard_map/ppermute | solution.py:22
  369.7 147.7 %collective-permute-start.8 = (bf16[2,512,1024]{2,1,0:T(8,128)(2,1)}, bf16[2,512,1024]{2,1,0:T(8,128)(2,1)}, u32[]{:S(2)}, u32[]{:S(2)}) collective-permute-start(bf16[2,512,1024]{2,1,0:T(8,128)(2,1)} %get-tuple-element.43), channel_id=1, source_target_pairs={{1,0},{2,1},{3,2},{4,3},{5,4},{6,5},{7,6},{8,7},{9,8},{10,9},{11,1... | collective-permute-start | bytes 6291464 | tf_op jit(solution)/shard_map/ppermute | solution.py:22
  478.9 207.9 %collective-permute-start.37 = (bf16[2,2,2,2,32,4096]{5,4,0,3,1,2:T(8,128)(2,1)}, bf16[2,2,2,2,32,4096]{5,4,0,3,1,2:T(8,128)(2,1)}, u32[]{:S(2)}, u32[]{:S(2)}) collective-permute-start(bf16[2,2,2,2,32,4096]{5,4,0,3,1,2:T(8,128)(2,1)} %bitcast.238), channel_id=1, source_target_pairs={{0,1},{1,0},{2,3},{3,2},{4,5},{5,4},{6,7},{7,6},{8,9},{9,8},{10,11... | collective-permute-start | bytes 12582920 | tf_op jit(solution)/shard_map/ppermute | solution.py:81
  497.8 12.4 %slice-start = ((s8[8388608]{0:T(1024)(128)(4,1)}), s8[4194304]{0:T(1024)(128)(4,1)S(1)}, s32[]{:S(2)}) async-start(s8[8388608]{0:T(1024)(128)(4,1)} %bitcast.264), calls=%async_computation.4 | async-start | bytes 8388608
  500.6 9.7 %slice-start.1 = ((s8[8388608]{0:T(1024)(128)(4,1)}), s8[4194304]{0:T(1024)(128)(4,1)S(1)}, s32[]{:S(2)}) async-start(s8[8388608]{0:T(1024)(128)(4,1)} %bitcast.264), calls=%async_computation.5 | async-start | bytes 8388608
  516.1 184.4 %collective-permute-start.42 = (bf16[2,2,2,2,128,1024]{5,4,0,1,2,3:T(8,128)(2,1)}, bf16[2,2,2,2,128,1024]{5,4,0,1,2,3:T(8,128)(2,1)}, u32[]{:S(2)}, u32[]{:S(2)}) collective-permute-start(bf16[2,2,2,2,128,1024]{5,4,0,1,2,3:T(8,128)(2,1)} %bitcast.237), channel_id=1, source_target_pairs={{0,1},{1,0},{2,3},{3,2},{4,5},{5,4},{6,7},{7,6},{8,9},{9,8},{10,11... | collective-permute-start | bytes 12582920 | tf_op jit(solution)/shard_map/ppermute | solution.py:81
  546.4 44.5 %copy-start.21 = (bf16[512,1024]{1,0:T(8,128)(2,1)S(1)}, bf16[512,1024]{1,0:T(8,128)(2,1)}, u32[]{:S(2)}) copy-start(bf16[512,1024]{1,0:T(8,128)(2,1)} %copy-done.20) | copy-start | bytes 3145732
  546.4 3.2 collective-permute-start.27
  549.7 42.9 %collective-permute-start.28 = (f32[2,2,2,1,384]{4,3,2,1,0:T(1,128)S(1)}, f32[2,2,2,1,384]{4,3,2,1,0:T(1,128)S(1)}, u32[]{:S(2)}, u32[]{:S(2)}) collective-permute-start(f32[2,2,2,1,384]{4,3,2,1,0:T(1,128)S(1)} %fusion.95), channel_id=1, source_target_pairs={{0,2},{1,3},{2,0},{3,1},{4,6},{5,7},{6,4},{7,5},{8,10},{9,11},{10,... | collective-permute-start | bytes 36872 | tf_op jit(solution)/shard_map/ppermute | solution.py:81
  592.7 35.9 %copy-start.22 = (bf16[1024,1024]{1,0:T(8,128)(2,1)S(1)}, bf16[1024,1024]{1,0:T(8,128)(2,1)}, u32[]{:S(2)}) copy-start(bf16[1024,1024]{1,0:T(8,128)(2,1)} %convolution_convert_fusion.2) | copy-start | bytes 6291460
  592.7 29.9 %collective-permute-start.29 = (f32[2,2,1,384]{3,2,1,0:T(1,128)S(1)}, f32[2,2,1,384]{3,2,1,0:T(1,128)S(1)}, u32[]{:S(2)}, u32[]{:S(2)}) collective-permute-start(f32[2,2,1,384]{3,2,1,0:T(1,128)S(1)} %fusion.98), channel_id=1, source_target_pairs={{0,4},{1,5},{2,6},{3,7},{4,0},{5,1},{6,2},{7,3},{8,12},{9,13},{10,... | collective-permute-start | bytes 18440 | tf_op jit(solution)/shard_map/ppermute | solution.py:81
  622.5 7.6 collective-permute-start.30
  629.5 15.3 %collective-permute-start.22 = (bf16[2,2,2,2,32,1024]{5,4,0,2,3,1:T(8,128)(2,1)S(1)}, bf16[2,2,2,2,32,1024]{5,4,0,2,3,1:T(8,128)(2,1)S(1)}, u32[]{:S(2)}, u32[]{:S(2)}) collective-permute-start(bf16[2,2,2,2,32,1024]{5,4,0,2,3,1:T(8,128)(2,1)S(1)} %bitcast.254), channel_id=1, source_target_pairs={{0,1},{1,0},{2,3},{3,2},{4,5},{5,4},{6,7},{7,6},{8,9},{9,8},{10,11... | collective-permute-start | bytes 3145736 | tf_op jit(solution)/shard_map/ppermute | solution.py:81
  630.2 12.8 %collective-permute-start.31 = (f32[1,384]{1,0:T(1,128)S(1)}, f32[1,384]{1,0:T(1,128)S(1)}, u32[]{:S(2)}, u32[]{:S(2)}) collective-permute-start(f32[1,384]{1,0:T(1,128)S(1)} %fusion.104), channel_id=1, source_target_pairs={{0,16},{1,17},{2,18},{3,19},{4,20},{5,21},{6,22},{7,23},{8,24},{9,... | collective-permute-start | bytes 4616 | tf_op jit(solution)/shard_map/ppermute | solution.py:81
  642.3 3.3 collective-permute-start.17
  643.0 4.0 collective-permute-start.12
  643.8 153.2 %copy-start.37 = (f32[32]{0:T(128)}, f32[32]{0:T(128)S(1)}, u32[]{:S(2)}) copy-start(f32[32]{0:T(128)S(1)} %get-tuple-element.118) | copy-start | bytes 388
  644.8 4.3 collective-permute-start.32
  645.6 14.1 %collective-permute-start.23 = (bf16[2,2,2,32,1024]{4,3,0,1,2:T(8,128)(2,1)S(1)}, bf16[2,2,2,32,1024]{4,3,0,1,2:T(8,128)(2,1)S(1)}, u32[]{:S(2)}, u32[]{:S(2)}) collective-permute-start(bf16[2,2,2,32,1024]{4,3,0,1,2:T(8,128)(2,1)S(1)} %fusion.70), channel_id=1, source_target_pairs={{0,8},{1,9},{2,10},{3,11},{4,12},{5,13},{6,14},{7,15},{8,0},{9,1},... | collective-permute-start | bytes 1572872 | tf_op jit(solution)/shard_map/ppermute | solution.py:81
  647.0 13.8 %collective-permute-start.18 = (bf16[2,2,2,32,1024]{4,3,0,2,1:T(8,128)(2,1)S(1)}, bf16[2,2,2,32,1024]{4,3,0,2,1:T(8,128)(2,1)S(1)}, u32[]{:S(2)}, u32[]{:S(2)}) collective-permute-start(bf16[2,2,2,32,1024]{4,3,0,2,1:T(8,128)(2,1)S(1)} %fusion.69), channel_id=1, source_target_pairs={{0,4},{1,5},{2,6},{3,7},{4,0},{5,1},{6,2},{7,3},{8,12},{9,13},{10,... | collective-permute-start | bytes 1572872 | tf_op jit(solution)/shard_map/ppermute | solution.py:81
  649.1 14.0 %collective-permute-start.13 = (bf16[2,2,2,32,1024]{4,3,0,1,2:T(8,128)(2,1)S(1)}, bf16[2,2,2,32,1024]{4,3,0,1,2:T(8,128)(2,1)S(1)}, u32[]{:S(2)}, u32[]{:S(2)}) collective-permute-start(bf16[2,2,2,32,1024]{4,3,0,1,2:T(8,128)(2,1)S(1)} %fusion.68), channel_id=1, source_target_pairs={{0,2},{1,3},{2,0},{3,1},{4,6},{5,7},{6,4},{7,5},{8,10},{9,11},{10,... | collective-permute-start | bytes 1572872 | tf_op jit(solution)/shard_map/ppermute | solution.py:81
  659.7 14.9 %collective-permute-start.33 = (bf16[2,2,2,32,1024]{4,3,0,1,2:T(8,128)(2,1)S(1)}, bf16[2,2,2,32,1024]{4,3,0,1,2:T(8,128)(2,1)S(1)}, u32[]{:S(2)}, u32[]{:S(2)}) collective-permute-start(bf16[2,2,2,32,1024]{4,3,0,1,2:T(8,128)(2,1)S(1)} %fusion.71), channel_id=1, source_target_pairs={{0,8},{1,9},{2,10},{3,11},{4,12},{5,13},{6,14},{7,15},{8,0},{9,1},... | collective-permute-start | bytes 1572872 | tf_op jit(solution)/shard_map/ppermute | solution.py:81
  660.8 16.0 %collective-permute-start.24 = (bf16[2,2,32,1024]{3,2,0,1:T(8,128)(2,1)S(1)}, bf16[2,2,32,1024]{3,2,0,1:T(8,128)(2,1)S(1)}, u32[]{:S(2)}, u32[]{:S(2)}) collective-permute-start(bf16[2,2,32,1024]{3,2,0,1:T(8,128)(2,1)S(1)} %fusion.76), channel_id=1, source_target_pairs={{0,2},{1,3},{2,0},{3,1},{4,6},{5,7},{6,4},{7,5},{8,10},{9,11},{10,... | collective-permute-start | bytes 786440 | tf_op jit(solution)/shard_map/ppermute | solution.py:81
  663.1 15.9 %collective-permute-start.19 = (bf16[2,2,32,1024]{3,2,0,1:T(8,128)(2,1)S(1)}, bf16[2,2,32,1024]{3,2,0,1:T(8,128)(2,1)S(1)}, u32[]{:S(2)}, u32[]{:S(2)}) collective-permute-start(bf16[2,2,32,1024]{3,2,0,1:T(8,128)(2,1)S(1)} %fusion.75), channel_id=1, source_target_pairs={{0,8},{1,9},{2,10},{3,11},{4,12},{5,13},{6,14},{7,15},{8,0},{9,1},... | collective-permute-start | bytes 786440 | tf_op jit(solution)/shard_map/ppermute | solution.py:81
  674.6 7.4 collective-permute-start.14
  676.8 7.8 collective-permute-start.34
  679.0 5.7 collective-permute-start.25
  680.6 9.0 %copy-start.10 = (bf16[2,2,2,2,1,32,4096]{6,5,4,3,2,1,0:T(8,128)(2,1)S(1)}, bf16[2,2,2,2,1,32,4096]{6,5,4,3,2,1,0:T(8,128)(2,1)}, u32[]{:S(2)}) copy-start(bf16[2,2,2,2,1,32,4096]{6,5,4,3,2,1,0:T(8,128)(2,1)} %get-tuple-element.49) | copy-start | bytes 12582916
  682.0 13.0 %collective-permute-start.20 = (bf16[2,32,1024]{2,1,0:T(8,128)(2,1)S(1)}, bf16[2,32,1024]{2,1,0:T(8,128)(2,1)S(1)}, u32[]{:S(2)}, u32[]{:S(2)}) collective-permute-start(bf16[2,32,1024]{2,1,0:T(8,128)(2,1)S(1)} %fusion.82), channel_id=1, source_target_pairs={{0,2},{1,3},{2,0},{3,1},{4,6},{5,7},{6,4},{7,5},{8,10},{9,11},{10,... | collective-permute-start | bytes 393224 | tf_op jit(solution)/shard_map/ppermute | solution.py:81
  684.7 10.6 %collective-permute-start.15 = (bf16[2,32,1024]{2,1,0:T(8,128)(2,1)S(1)}, bf16[2,32,1024]{2,1,0:T(8,128)(2,1)S(1)}, u32[]{:S(2)}, u32[]{:S(2)}) collective-permute-start(bf16[2,32,1024]{2,1,0:T(8,128)(2,1)S(1)} %fusion.81), channel_id=1, source_target_pairs={{0,8},{1,9},{2,10},{3,11},{4,12},{5,13},{6,14},{7,15},{8,0},{9,1},... | collective-permute-start | bytes 393224 | tf_op jit(solution)/shard_map/ppermute | solution.py:81
  684.8 10.9 %collective-permute-start.35 = (bf16[2,32,1024]{2,1,0:T(8,128)(2,1)S(1)}, bf16[2,32,1024]{2,1,0:T(8,128)(2,1)S(1)}, u32[]{:S(2)}, u32[]{:S(2)}) collective-permute-start(bf16[2,32,1024]{2,1,0:T(8,128)(2,1)S(1)} %fusion.84), channel_id=1, source_target_pairs={{0,4},{1,5},{2,6},{3,7},{4,0},{5,1},{6,2},{7,3},{8,12},{9,13},{10,... | collective-permute-start | bytes 393224 | tf_op jit(solution)/shard_map/ppermute | solution.py:81
  686.7 11.9 %collective-permute-start.26 = (bf16[32,1024]{1,0:T(8,128)(2,1)S(1)}, bf16[32,1024]{1,0:T(8,128)(2,1)S(1)}, u32[]{:S(2)}, u32[]{:S(2)}) collective-permute-start(bf16[32,1024]{1,0:T(8,128)(2,1)S(1)} %fusion.88), channel_id=1, source_target_pairs={{0,16},{1,17},{2,18},{3,19},{4,20},{5,21},{6,22},{7,23},{8,24},{9,... | collective-permute-start | bytes 196616 | tf_op jit(solution)/shard_map/ppermute | solution.py:81
  695.0 44.6 %collective-permute-start.38 = (bf16[2,2,2,32,4096]{4,3,0,2,1:T(8,128)(2,1)}, bf16[2,2,2,32,4096]{4,3,0,2,1:T(8,128)(2,1)}, u32[]{:S(2)}, u32[]{:S(2)}) collective-permute-start(bf16[2,2,2,32,4096]{4,3,0,2,1:T(8,128)(2,1)} %fusion.35), channel_id=1, source_target_pairs={{0,4},{1,5},{2,6},{3,7},{4,0},{5,1},{6,2},{7,3},{8,12},{9,13},{10,... | collective-permute-start | bytes 6291464 | tf_op jit(solution)/shard_map/ppermute | solution.py:81
  695.3 5.2 collective-permute-start.21
  695.6 47.3 %collective-permute-start.16 = (bf16[32,1024]{1,0:T(8,128)(2,1)S(1)}, bf16[32,1024]{1,0:T(8,128)(2,1)S(1)}, u32[]{:S(2)}, u32[]{:S(2)}) collective-permute-start(bf16[32,1024]{1,0:T(8,128)(2,1)S(1)} %fusion.86), channel_id=1, source_target_pairs={{0,16},{1,17},{2,18},{3,19},{4,20},{5,21},{6,22},{7,23},{8,24},{9,... | collective-permute-start | bytes 196616 | tf_op jit(solution)/shard_map/ppermute | solution.py:81
  698.6 67.8 %collective-permute-start.36 = (bf16[32,1024]{1,0:T(8,128)(2,1)S(1)}, bf16[32,1024]{1,0:T(8,128)(2,1)S(1)}, u32[]{:S(2)}, u32[]{:S(2)}) collective-permute-start(bf16[32,1024]{1,0:T(8,128)(2,1)S(1)} %fusion.89), channel_id=1, source_target_pairs={{0,16},{1,17},{2,18},{3,19},{4,20},{5,21},{6,22},{7,23},{8,24},{9,... | collective-permute-start | bytes 196616 | tf_op jit(solution)/shard_map/ppermute | solution.py:81
  705.0 44.7 %collective-permute-start.43 = (bf16[2,2,2,128,1024]{4,3,0,1,2:T(8,128)(2,1)S(1)}, bf16[2,2,2,128,1024]{4,3,0,1,2:T(8,128)(2,1)S(1)}, u32[]{:S(2)}, u32[]{:S(2)}) collective-permute-start(bf16[2,2,2,128,1024]{4,3,0,1,2:T(8,128)(2,1)S(1)} %fusion.36), channel_id=1, source_target_pairs={{0,2},{1,3},{2,0},{3,1},{4,6},{5,7},{6,4},{7,5},{8,10},{9,11},{10,... | collective-permute-start | bytes 6291464 | tf_op jit(solution)/shard_map/ppermute | solution.py:81
  742.0 21.0 %collective-permute-start.39 = (bf16[2,2,32,4096]{3,2,0,1:T(8,128)(2,1)S(1)}, bf16[2,2,32,4096]{3,2,0,1:T(8,128)(2,1)S(1)}, u32[]{:S(2)}, u32[]{:S(2)}) collective-permute-start(bf16[2,2,32,4096]{3,2,0,1:T(8,128)(2,1)S(1)} %fusion.63), channel_id=1, source_target_pairs={{0,8},{1,9},{2,10},{3,11},{4,12},{5,13},{6,14},{7,15},{8,0},{9,1},... | collective-permute-start | bytes 3145736 | tf_op jit(solution)/shard_map/ppermute | solution.py:81
  750.6 21.2 %collective-permute-start.44 = (bf16[2,2,128,1024]{3,2,0,1:T(8,128)(2,1)S(1)}, bf16[2,2,128,1024]{3,2,0,1:T(8,128)(2,1)S(1)}, u32[]{:S(2)}, u32[]{:S(2)}) collective-permute-start(bf16[2,2,128,1024]{3,2,0,1:T(8,128)(2,1)S(1)} %fusion.64), channel_id=1, source_target_pairs={{0,4},{1,5},{2,6},{3,7},{4,0},{5,1},{6,2},{7,3},{8,12},{9,13},{10,... | collective-permute-start | bytes 3145736 | tf_op jit(solution)/shard_map/ppermute | solution.py:81
  763.3 11.0 %collective-permute-start.40 = (bf16[2,32,4096]{2,1,0:T(8,128)(2,1)S(1)}, bf16[2,32,4096]{2,1,0:T(8,128)(2,1)S(1)}, u32[]{:S(2)}, u32[]{:S(2)}) collective-permute-start(bf16[2,32,4096]{2,1,0:T(8,128)(2,1)S(1)} %fusion.72), channel_id=1, source_target_pairs={{0,2},{1,3},{2,0},{3,1},{4,6},{5,7},{6,4},{7,5},{8,10},{9,11},{10,... | collective-permute-start | bytes 1572872 | tf_op jit(solution)/shard_map/ppermute | solution.py:81
  772.1 14.2 %collective-permute-start.45 = (bf16[2,128,1024]{2,1,0:T(8,128)(2,1)S(1)}, bf16[2,128,1024]{2,1,0:T(8,128)(2,1)S(1)}, u32[]{:S(2)}, u32[]{:S(2)}) collective-permute-start(bf16[2,128,1024]{2,1,0:T(8,128)(2,1)S(1)} %fusion.73), channel_id=1, source_target_pairs={{0,8},{1,9},{2,10},{3,11},{4,12},{5,13},{6,14},{7,15},{8,0},{9,1},... | collective-permute-start | bytes 1572872 | tf_op jit(solution)/shard_map/ppermute | solution.py:81
  774.5 13.3 %collective-permute-start.41 = (bf16[32,4096]{1,0:T(8,128)(2,1)S(1)}, bf16[32,4096]{1,0:T(8,128)(2,1)S(1)}, u32[]{:S(2)}, u32[]{:S(2)}) collective-permute-start(bf16[32,4096]{1,0:T(8,128)(2,1)S(1)} %fusion.78), channel_id=1, source_target_pairs={{0,16},{1,17},{2,18},{3,19},{4,20},{5,21},{6,22},{7,23},{8,24},{9,... | collective-permute-start | bytes 786440 | tf_op jit(solution)/shard_map/ppermute | solution.py:81
  786.5 9.6 %collective-permute-start.46 = (bf16[128,1024]{1,0:T(8,128)(2,1)S(1)}, bf16[128,1024]{1,0:T(8,128)(2,1)S(1)}, u32[]{:S(2)}, u32[]{:S(2)}) collective-permute-start(bf16[128,1024]{1,0:T(8,128)(2,1)S(1)} %fusion.79), channel_id=1, source_target_pairs={{0,16},{1,17},{2,18},{3,19},{4,20},{5,21},{6,22},{7,23},{8,24},{9,... | collective-permute-start | bytes 786440 | tf_op jit(solution)/shard_map/ppermute | solution.py:81
  (28 other events, 123.6 us)
Sparse Core Ops, SparseCore 0:
  15.1 59.9 all-gather.4
  78.0 68.3 all-gather.6
  149.3 174.9 all-gather.8
  327.0 96.0 all-gather.10

commit v2 on v1

--- a/solution.py
+++ b/solution.py
@@ -66,21 +66,29 @@
     return rows * stay + sign * (behind * upper - ahead * lower)
 
 
-def owned_sum(parts, axis, order, send_type):
+def halved(held, left, bit, axis, send_type):
     devices = lax.axis_size(axis)
-    place = lax.axis_index(axis)
+    where = left.index(bit)
+    mine = (lax.axis_index(axis) >> bit) & 1
+    sent = lax.dynamic_index_in_dim(held, 1 - mine, where, keepdims=False)
+    kept = lax.dynamic_index_in_dim(held, mine, where, keepdims=False)
+    route = [(i, i ^ (1 << bit)) for i in range(devices)]
+    got = lax.ppermute(sent.astype(send_type), axis, route)
+    left.remove(bit)
+    return kept.astype(jnp.float32) + got.astype(jnp.float32)
+
+
+def by_owner(parts, axis):
+    devices = lax.axis_size(axis)
     bits = devices.bit_length() - 1
     held = parts.reshape((2,) * bits + (parts.shape[0] // devices,) + parts.shape[1:])
-    left = list(range(bits - 1, -1, -1))
+    return held, list(range(bits - 1, -1, -1))
+
+
+def owned_sum(parts, axis, order, send_type):
+    held, left = by_owner(parts, axis)
     for bit in order:
-        where = left.index(bit)
-        mine = (place >> bit) & 1
-        sent = lax.dynamic_index_in_dim(held, 1 - mine, where, keepdims=False)
-        kept = lax.dynamic_index_in_dim(held, mine, where, keepdims=False)
-        route = [(i, i ^ (1 << bit)) for i in range(devices)]
-        got = lax.ppermute(sent.astype(send_type), axis, route)
-        held = kept.astype(jnp.float32) + got.astype(jnp.float32)
-        left.remove(bit)
+        held = halved(held, left, bit, axis, send_type)
     return held
 
 
@@ -318,18 +326,23 @@
     )
     columns = jnp.concatenate([entry.reshape(share, -1) for entry in vectors], axis=1)
     columns = jnp.pad(columns, ((0, 0), (0, 128 - columns.shape[1])))
-    dense_wide = gather(jnp.concatenate([dense_weight, columns], axis=1))
-    dense_full = dense_wide[:, :features]
+    lower_rows = lower_weight.reshape(share, -1)
+    weights = (dense_weight, qkv_weight, upper_weight, lower_rows, columns)
+    wide = gather(jnp.concatenate(weights, axis=1))
+    fulls = []
+    at = 0
+    for entry in weights:
+        fulls.append(wide[:, at : at + entry.shape[1]])
+        at += entry.shape[1]
+    dense_full, qkv_full, upper_full, lower_full, columns = fulls
+    lower_full = lower_full.reshape(-1, features)
     rows_out = []
-    at = features
+    at = 0
     for entry in vectors:
         width = entry.shape[0] // share
-        rows_out.append(dense_wide[:, at : at + width].reshape(-1).astype(f32))
+        rows_out.append(columns[:, at : at + width].reshape(-1).astype(f32))
         at += width
     qkv_row, dense_row, upper_row, lower_row, gain_attn, shift_attn, gain_mlp, shift_mlp = rows_out
-    qkv_full = gather(qkv_weight)
-    upper_full = gather(upper_weight)
-    lower_full = gather(lower_weight)
 
     segment_plus = segment_ids + 1
     earlier = [shifted(segment_plus, "fsdp", distance) for distance in range(reach_devices, 0, -1)]
@@ -354,14 +367,6 @@
     grad_attended = jnp.einsum("te,de->td", cotangent, dense_full, preferred_element_type=f32)
     grad_attended = grad_attended.astype(jnp.bfloat16)
 
-    attended, grad_query, grad_pairs = attention(
-        first, segment_plus, ext_segment, query_rot, grad_attended, ext_pairs
-    )
-    returned = [
-        shifted(grad_pairs[reach_devices - distance], "fsdp", -distance)
-        for distance in range(1, reach_devices + 1)
-    ]
-
     normed_mlp, normal_mlp, inverse_mlp = layer_norm(hidden_f, gain_mlp, shift_mlp)
     normed_mlp = normed_mlp.astype(jnp.bfloat16)
     upper = jnp.dot(normed_mlp, upper_full, preferred_element_type=f32) + upper_row
@@ -371,19 +376,45 @@
     low = jnp.bfloat16
     cotangent_f = cotangent.astype(f32)
 
-    def weight_grad(left, right, turn):
-        product = lax.dot_general(
+    def product(left, right):
+        return lax.dot_general(
             left, right, (((0,), (0,)), ((), ())), preferred_element_type=f32
         ).astype(low)
-        order = sum_order(devices, turn)
-        return owned_sum(product, "fsdp", order, low)
-
-    lower_weight_grad = weight_grad(active, cotangent, 0)
+
+    def summed(term, turn):
+        return owned_sum(term, "fsdp", sum_order(devices, turn), low)
+
+    def weight_grad(left, right, turn):
+        return summed(product(left, right), turn)
+
+    lower_term = product(active, cotangent)
     grad_active = jnp.einsum("td,fd->tf", cotangent, lower_full, preferred_element_type=f32)
     grad_upper = gelu_pull(grad_active)[0].astype(low)
-    upper_weight_grad = weight_grad(normed_mlp, grad_upper, 1)
+    upper_term = product(normed_mlp, grad_upper)
+    mlp_branch = jnp.dot(active, lower_full, preferred_element_type=f32) + lower_row
+    lower_order = sum_order(devices, 0)
+    upper_order = sum_order(devices, 1)
+    lower_held, lower_left = by_owner(lower_term, "fsdp")
+    upper_held, upper_left = by_owner(upper_term, "fsdp")
+    lower_held = halved(lower_held, lower_left, lower_order[0], "fsdp", low)
+    upper_held = halved(upper_held, upper_left, upper_order[0], "fsdp", low)
+    query_rot, lower_held, upper_held, mlp_branch = lax.optimization_barrier(
+        (query_rot, lower_held, upper_held, mlp_branch)
+    )
+    for bit in lower_order[1:]:
+        lower_held = halved(lower_held, lower_left, bit, "fsdp", low)
+    for bit in upper_order[1:]:
+        upper_held = halved(upper_held, upper_left, bit, "fsdp", low)
+
+    attended, grad_query, grad_pairs = attention(
+        first, segment_plus, ext_segment, query_rot, grad_attended, ext_pairs
+    )
+    returned = [
+        shifted(grad_pairs[reach_devices - distance], "fsdp", -distance)
+        for distance in range(1, reach_devices + 1)
+    ]
+
     dense_weight_grad = weight_grad(attended, cotangent, 2)
-    mlp_branch = jnp.dot(active, lower_full, preferred_element_type=f32) + lower_row
     attn_branch = jnp.dot(attended, dense_full, preferred_element_type=f32) + dense_row
     hidden_out = (hidden_f + attn_branch + mlp_branch).astype(jnp.bfloat16)
     column_sums = jnp.sum(cotangent_f, axis=0)
@@ -440,9 +471,9 @@
         pieces[0],
         dense_weight_grad,
         pieces[1],
-        upper_weight_grad,
+        upper_held,
         pieces[2],
-        lower_weight_grad,
+        lower_held,
         pieces[1],
         pieces[3],
         pieces[4],

time: 811 us -> 890 us (1.097)
  starting transfers between devices: 164 us -> 230 us
  local copies, waits for them, and re-layouts: 84.2 us -> 109 us
  waiting for transfers between devices: 357 us -> 336 us
    ppermute x35, starting transfers between devices: 129 us -> 198 us  [halved(): got = lax.ppermute(sent.astype(send_type), axis, route)]
    ppermute x12, waiting for transfers between devices: 131 us -> 114 us  [shifted(): return lax.ppermute(block, axis, route)]
    dot_general x1, matrix products: 10.3 us -> 26 us  [on_device(): jnp.dot(normed_mlp, upper_full, preferred_element_type=f32) + upper_row]
    reshape x0 -> x2, local copies, waits for them, and re-layouts: none -> 15.1 us  [the longest x1 13.9 us: on_device(): lower_full = lower_full.reshape(-1, features)]
    dot_general x1, matrix products: 27.9 us -> 14.4 us  [on_device(): jnp.einsum('td,fd->tf', cotangent, lower_full, preferred_element_type=f32)]
    convert_element_type x4 -> x3, other arithmetic: 16.2 us -> 6.46 us  [on_device(): rows_out.append(columns[:, at:at + width].reshape(-1).astype(f32))]
    all_gather x4 -> x1, waiting for transfers between devices: 127 us -> 129 us  [gather(): return lax.all_gather(shard, 'fsdp', axis=0, tiled=True)]
    unnamed x91 -> x97, local copies, waits for them, and re-layouts: 18.4 us -> 16.7 us
  transfers between devices with their start and end apart: 51 -> 48, of which waited for: 22 -> 20; matrix products, arithmetic and copies ran while one was open for 28% -> 21% of each run, Pallas kernels for 3% -> 0%
where the time goes in v2:
time: 890 us; the launch traced here: 879 us
  waiting for transfers between devices  336 us (38%)
  starting transfers between devices  230 us (26%)
  local copies, waits for them, and re-layouts  109 us (12%)
  matrix products  102 us (11%)
  other arithmetic  58.4 us (7%)
  Pallas kernels  27.7 us (3%)
  between operations  15.7 us (2%)
    ppermute x35, starting transfers between devices, halved(): got = lax.ppermute(sent.astype(send_type), axis, route)  198 us
    all_gather x1, waiting for transfers between devices, gather(): return lax.all_gather(shard, 'fsdp', axis=0, tiled=True)  129 us
    ppermute x12, waiting for transfers between devices, shifted(): return lax.ppermute(block, axis, route)  114 us
    ppermute x35, waiting for transfers between devices, halved(): got = lax.ppermute(sent.astype(send_type), axis, route)  92.9 us
    ppermute x12, starting transfers between devices, shifted(): return lax.ppermute(block, axis, route)  31.9 us
    pallas_call x1, Pallas kernels, attention(): pl.pallas_call(attention_kernel, out_shape=(jax.ShapeDtypeStruct((rows, f...  27.7 us
    dot_general x1, matrix products, on_device(): jnp.dot(normed_mlp, upper_full, preferred_element_type=f32) + upper_row  26 us
    add x35, other arithmetic, halved(): return kept.astype(jnp.float32) + got.astype(jnp.float32)  24.2 us
  transfers between devices with their start and end apart: 48, of which 20 were waited for; matrix products, arithmetic and copies ran while one was open for 21% of the time, Pallas kernels for 0%

profile of v2, /device:TPU:0, one launch (start us, length us, event | category | flops | bytes accessed | tf_op | source)
XLA Modules:
  0.0 879.1 jit_solution(7380867792691725828)
XLA Ops:
  18.3 2.4 collective-permute-start.3
  20.7 4.4 collective-permute-start.2
  25.1 4.3 collective-permute-start.1
  29.4 3.4 collective-permute-start
  40.7 2.9 copy.86
  45.2 3.0 copy.87
  48.2 128.9 %all-gather.2.cloned.1.call-done = bf16[1024,12416]{1,0:T(8,128)(2,1)} async-done(((bf16[32,12416]{1,0:T(8,128)(2,1)}), bf16[1024,12416]{1,0:T(8,128)(2,1)}) %all-gather.2.cloned.1.call-update) | async-done | bytes 25427984 | tf_op jit(solution)/shard_map/all_gather | solution.py:315
  180.2 3.6 convert_reduce_fusion.5
  183.8 5.8 fusion.21
  192.6 4.6 fusion.127
  198.5 7.7 slice.267
  206.3 13.9 %reshape.280 = bf16[4096,1024]{1,0:T(8,128)(2,1)} reshape(bf16[1024,4096]{1,0:T(8,128)(2,1)} %slice.267) | data formatting | bytes 16777216 | tf_op jit(solution)/shard_map/reshape | solution.py:338
  220.2 7.2 fusion.56
  228.4 4.9 collective-permute-start.6
  233.3 26.0 %multiply_convert_fusion = (bf16[512,4096]{1,0:T(8,128)(2,1)S(1)}, f32[512,4096]{1,0:T(8,128)}, f32[512,4096]{1,0:T(8,128)}) fusion(f32[4096]{0:T(1024)S(1)} %reshape.291, bf16[1024,12416]{1,0:T(8,128)(2,1)} %all-gather.2.cloned.1.call-done, bf16[512,1024]{1,0:T(8,128)(2,1)S(1)} %copy-done.12, f32[1024]{0:T(1024)S(1)} %get-tuple-element.30, ...), kind=kOutput, calls=%fused_computation.14 | convolution fusion | flops 4436525056 | bytes 30437376 | tf_op jit(solution)/shard_map/dot_general | solution.py:372
  259.3 6.8 convolution_convert_fusion.1
  266.1 6.9 constant_dynamic-slice_fusion.19
  273.0 2.8 copy.144
  275.8 14.4 %convert_reduce_fusion = (f32[4096]{0:T(1024)}, bf16[512,4096]{1,0:T(8,128)(2,1)S(1)}) fusion(f32[512,4096]{1,0:T(8,128)} %get-tuple-element.47, bf16[4096,1024]{1,0:T(8,128)(2,1)} %reshape.280, bf16[512,1024]{1,0:T(8,128)(2,1)S(1)} %copy-done.19, f32[512,4096]{1,0:T(8,128)} %get-tuple-element.94, f32[4096]{0:T(1024)S(1)} %reshape.291), kind=kOutput, calls=%fused_computation.13 | convolution fusion | flops 4330614784 | bytes 30441472 | tf_op jit(solution)/shard_map/td,fd->tf/dot_general | solution.py:391
  290.2 7.2 convolution_convert_fusion
  297.4 6.3 constant_dynamic-slice_fusion.17
  303.7 2.4 copy.143
  309.9 3.9 fusion.118
  313.9 2.3 collective-permute-start.9
  318.3 3.1 fusion.77.grad_ref
  321.4 2.6 collective-permute-start.8
  324.1 8.6 convolution_add_fusion
  334.5 29.7 %collective-permute-done.7 = bf16[512,2048]{1,0:T(8,128)(2,1)S(1)} collective-permute-done((bf16[512,2048]{1,0:T(8,128)(2,1)S(1)}, bf16[512,2048]{1,0:T(8,128)(2,1)S(1)}, u32[]{:S(2)}, u32[]{:S(2)}) %collective-permute-start.7) | collective-permute-done | bytes 2097184 | tf_op jit(solution)/shard_map/ppermute | solution.py:22
  364.4 42.5 %collective-permute-done.8 = bf16[512,2048]{1,0:T(8,128)(2,1)S(1)} collective-permute-done((bf16[512,2048]{1,0:T(8,128)(2,1)S(1)}, bf16[512,2048]{1,0:T(8,128)(2,1)S(1)}, u32[]{:S(2)}, u32[]{:S(2)}) %collective-permute-start.8) | collective-permute-done | bytes 2097184 | tf_op jit(solution)/shard_map/ppermute | solution.py:22
  409.0 4.7 copy-done.22
  413.7 7.5 convert_add_fusion.1
  421.3 5.1 convert_add_fusion
  426.3 27.7 %shard_map.254 = (bf16[512,1024]{1,0:T(8,128)(2,1)S(1)}, f32[512,1024]{1,0:T(8,128)S(1)}, bf16[5,2,512,1024]{3,2,1,0:T(8,128)(2,1)}) custom-call(s32[1]{0:T(128)} %bitcast.1.first_ref, s32[1,512]{1,0:T(1,128)S(1)} %bitcast.258, s32[2560,1]{1,0:T(8,128)S(1)} %broadcast_in_dim.12.key_segment_ref, bf16[512,1024]{1,0:T(8,128)(2,1)S(1)} %get-tuple-element.21.query_ref, ...), custom_call_target="tpu_custom_call" | custom-call | flops 80530636800 | bytes 62914560 | tf_op jit(solution)/shard_map/pallas_call | solution.py:256
  454.0 6.1 slice_bitcast_fusion.4
  465.7 10.5 %fusion.13 = f32[512,1024]{1,0:T(8,128)} fusion(bf16[512,4096]{1,0:T(8,128)(2,1)} %copy-done.39, bf16[1024,12416]{1,0:T(8,128)(2,1)} %all-gather.2.cloned.1.call-done), kind=kOutput, calls=%fused_computation.30 | convolution fusion | flops 4294967296 | bytes 14680064 | tf_op jit(solution)/shard_map/tf,df->td/dot_general | solution.py:422
  476.3 3.9 fusion.54
  480.2 42.4 %collective-permute-start.43 = (bf16[2,2,2,128,1024]{4,3,0,1,2:T(8,128)(2,1)}, bf16[2,2,2,128,1024]{4,3,0,1,2:T(8,128)(2,1)}, u32[]{:S(2)}, u32[]{:S(2)}) collective-permute-start(bf16[2,2,2,128,1024]{4,3,0,1,2:T(8,128)(2,1)} %fusion.54), channel_id=1, source_target_pairs={{0,2},{1,3},{2,0},{3,1},{4,6},{5,7},{6,4},{7,5},{8,10},{9,11},{10,... | collective-permute-start | bytes 6291464 | tf_op jit(solution)/shard_map/ppermute | solution.py:76
  523.4 2.6 convolution_convert_fusion.2
  526.0 4.2 fusion.70
  532.7 20.6 %collective-permute-start.39 = (bf16[2,2,2,32,4096]{4,3,0,2,1:T(8,128)(2,1)}, bf16[2,2,2,32,4096]{4,3,0,2,1:T(8,128)(2,1)}, u32[]{:S(2)}, u32[]{:S(2)}) collective-permute-start(bf16[2,2,2,32,4096]{4,3,0,2,1:T(8,128)(2,1)} %fusion.53), channel_id=1, source_target_pairs={{0,4},{1,5},{2,6},{3,7},{4,0},{5,1},{6,2},{7,3},{8,12},{9,13},{10,... | collective-permute-start | bytes 6291464 | tf_op jit(solution)/shard_map/ppermute | solution.py:76
  553.4 41.6 %collective-permute-done.11 = bf16[2,512,1024]{2,1,0:T(8,128)(2,1)} collective-permute-done((bf16[2,512,1024]{2,1,0:T(8,128)(2,1)}, bf16[2,512,1024]{2,1,0:T(8,128)(2,1)}, u32[]{:S(2)}, u32[]{:S(2)}) %collective-permute-start.11) | collective-permute-done | bytes 2097184 | tf_op jit(solution)/shard_map/ppermute | solution.py:22
  595.0 4.7 fusion.26
  604.0 2.8 fusion.65
  606.9 8.2 fusion.48
  615.8 5.7 convert_reduce_fusion.4
  623.8 12.4 %collective-permute-done.43 = bf16[2,2,2,128,1024]{4,3,0,1,2:T(8,128)(2,1)} collective-permute-done((bf16[2,2,2,128,1024]{4,3,0,1,2:T(8,128)(2,1)}, bf16[2,2,2,128,1024]{4,3,0,1,2:T(8,128)(2,1)}, u32[]{:S(2)}, u32[]{:S(2)}) %collective-permute-start.43) | collective-permute-done | bytes 2097184 | tf_op jit(solution)/shard_map/ppermute | solution.py:76
  636.3 3.6 bitcast_add_fusion
  641.3 19.8 %collective-permute-done.39 = bf16[2,2,2,32,4096]{4,3,0,2,1:T(8,128)(2,1)} collective-permute-done((bf16[2,2,2,32,4096]{4,3,0,2,1:T(8,128)(2,1)}, bf16[2,2,2,32,4096]{4,3,0,2,1:T(8,128)(2,1)}, u32[]{:S(2)}, u32[]{:S(2)}) %collective-permute-start.39) | collective-permute-done | bytes 2097184 | tf_op jit(solution)/shard_map/ppermute | solution.py:76
  661.1 2.3 bitcast_add_fusion.1
  665.0 75.0 %collective-permute-start.30 = (f32[2,2,2,1,384]{4,3,2,1,0:T(1,128)S(1)}, f32[2,2,2,1,384]{4,3,2,1,0:T(1,128)S(1)}, u32[]{:S(2)}, u32[]{:S(2)}) collective-permute-start(f32[2,2,2,1,384]{4,3,2,1,0:T(1,128)S(1)} %fusion.108), channel_id=1, source_target_pairs={{0,2},{1,3},{2,0},{3,1},{4,6},{5,7},{6,4},{7,5},{8,10},{9,11},{10,... | collective-permute-start | bytes 36872 | tf_op jit(solution)/shard_map/ppermute | solution.py:76
  740.1 2.5 collective-permute-start.44
  744.3 16.7 %collective-permute-start.40 = (bf16[2,2,32,4096]{3,2,0,1:T(8,128)(2,1)S(1)}, bf16[2,2,32,4096]{3,2,0,1:T(8,128)(2,1)S(1)}, u32[]{:S(2)}, u32[]{:S(2)}) collective-permute-start(bf16[2,2,32,4096]{3,2,0,1:T(8,128)(2,1)S(1)} %fusion.80), channel_id=1, source_target_pairs={{0,8},{1,9},{2,10},{3,11},{4,12},{5,13},{6,14},{7,15},{8,0},{9,1},... | collective-permute-start | bytes 3145736 | tf_op jit(solution)/shard_map/ppermute | solution.py:76
  761.1 4.8 collective-permute-done.31
  765.9 17.9 %collective-permute-start.32 = (f32[2,1,384]{2,1,0:T(1,128)S(1)}, f32[2,1,384]{2,1,0:T(1,128)S(1)}, u32[]{:S(2)}, u32[]{:S(2)}) collective-permute-start(f32[2,1,384]{2,1,0:T(1,128)S(1)} %fusion.114), channel_id=1, source_target_pairs={{0,8},{1,9},{2,10},{3,11},{4,12},{5,13},{6,14},{7,15},{8,0},{9,1},... | collective-permute-start | bytes 9224 | tf_op jit(solution)/shard_map/ppermute | solution.py:76
  792.5 2.1 collective-permute-start.45
  801.2 6.1 collective-permute-done.45
  810.0 14.1 %collective-permute-done.25 = bf16[2,2,2,32,1024]{4,3,0,1,2:T(8,128)(2,1)S(1)} collective-permute-done((bf16[2,2,2,32,1024]{4,3,0,1,2:T(8,128)(2,1)S(1)}, bf16[2,2,2,32,1024]{4,3,0,1,2:T(8,128)(2,1)S(1)}, u32[]{:S(2)}, u32[]{:S(2)}) %collective-permute-start.25) | collective-permute-done | bytes 524320 | tf_op jit(solution)/shard_map/ppermute | solution.py:76
  824.4 14.2 %collective-permute-done.35 = bf16[2,2,2,32,1024]{4,3,0,1,2:T(8,128)(2,1)S(1)} collective-permute-done((bf16[2,2,2,32,1024]{4,3,0,1,2:T(8,128)(2,1)S(1)}, bf16[2,2,2,32,1024]{4,3,0,1,2:T(8,128)(2,1)S(1)}, u32[]{:S(2)}, u32[]{:S(2)}) %collective-permute-start.35) | collective-permute-done | bytes 524320 | tf_op jit(solution)/shard_map/ppermute | solution.py:76
  841.6 6.2 collective-permute-done.26
  847.9 3.9 collective-permute-done.36
  857.3 2.3 collective-permute-start.28
  860.4 2.3 collective-permute-start.18
  863.5 3.2 collective-permute-done.28
  866.8 2.6 collective-permute-done.18
  (299 shorter events, 90.1 us)
Async XLA Ops:
  7.2 11.1 %copy-start.31 = (s32[512]{0:T(512)S(1)}, s32[512]{0:T(512)}, u32[]{:S(2)}) copy-start(s32[512]{0:T(512)} %param.17) | copy-start | bytes 6148
  7.2 25.7 %copy-start.11 = (bf16[512,1024]{1,0:T(8,128)(2,1)S(1)}, bf16[512,1024]{1,0:T(8,128)(2,1)}, u32[]{:S(2)}) copy-start(bf16[512,1024]{1,0:T(8,128)(2,1)} %param.15) | copy-start | bytes 3145732
  7.2 169.9 %all-gather.2.cloned.1.call-start = ((), (), s32[]{:S(2)}) async-start(), calls=%async_computation | async-start | bytes 26222592 | tf_op jit(solution)/shard_map/all_gather | solution.py:315
  18.3 15.9 %collective-permute-start.3 = (s32[512]{0:T(512)S(1)}, s32[512]{0:T(512)S(1)}, u32[]{:S(2)}, u32[]{:S(2)}) collective-permute-start(s32[512]{0:T(512)S(1)} %broadcast_add_fusion), channel_id=1, source_target_pairs={{0,1},{1,2},{2,3},{3,4},{4,5},{5,6},{6,7},{7,8},{8,9},{9,10},{10,1... | collective-permute-start | bytes 6152 | tf_op jit(solution)/shard_map/ppermute | solution.py:22
  20.7 13.5 %collective-permute-start.2 = (s32[512]{0:T(512)S(1)}, s32[512]{0:T(512)S(1)}, u32[]{:S(2)}, u32[]{:S(2)}) collective-permute-start(s32[512]{0:T(512)S(1)} %broadcast_add_fusion), channel_id=1, source_target_pairs={{0,2},{1,3},{2,4},{3,5},{4,6},{5,7},{6,8},{7,9},{8,10},{9,11},{10,... | collective-permute-start | bytes 6152 | tf_op jit(solution)/shard_map/ppermute | solution.py:22
  25.1 9.1 %collective-permute-start.1 = (s32[512]{0:T(512)S(1)}, s32[512]{0:T(512)S(1)}, u32[]{:S(2)}, u32[]{:S(2)}) collective-permute-start(s32[512]{0:T(512)S(1)} %broadcast_add_fusion), channel_id=1, source_target_pairs={{0,3},{1,4},{2,5},{3,6},{4,7},{5,8},{6,9},{7,10},{8,11},{9,12},{10... | collective-permute-start | bytes 6152 | tf_op jit(solution)/shard_map/ppermute | solution.py:22
  29.4 4.7 collective-permute-start
  33.1 257.0 %copy-start.23 = (f32[512]{0:T(512)}, f32[512]{0:T(512)S(1)}, u32[]{:S(2)}) copy-start(f32[512]{0:T(512)S(1)} %broadcast_multiply_fusion.5) | copy-start | bytes 6148
  33.5 256.6 %copy-start.32 = (f32[512]{0:T(512)}, f32[512]{0:T(512)S(1)}, u32[]{:S(2)}) copy-start(f32[512]{0:T(512)S(1)} %add_rsqrt_fusion) | copy-start | bytes 6148
  38.7 181.5 %copy-start.4 = (f32[512,1024]{1,0:T(8,128)}, f32[512,1024]{1,0:T(8,128)S(1)}, u32[]{:S(2)}) copy-start(f32[512,1024]{1,0:T(8,128)S(1)} %copy.88) | copy-start | bytes 6291460
  183.8 106.4 %copy-start.28 = (f32[1024]{0:T(1024)}, f32[1024]{0:T(1024)S(1)}, u32[]{:S(2)}) copy-start(f32[1024]{0:T(1024)S(1)} %get-tuple-element.31) | copy-start | bytes 12292
  189.6 7.5 copy-start
  228.4 93.0 %collective-permute-start.6 = (bf16[512,2048]{1,0:T(8,128)(2,1)S(1)}, bf16[512,2048]{1,0:T(8,128)(2,1)}, u32[]{:S(2)}, u32[]{:S(2)}) collective-permute-start(bf16[512,2048]{1,0:T(8,128)(2,1)S(1)} %pad_maximum_fusion.1), channel_id=1, source_target_pairs={{0,4},{1,5},{2,6},{3,7},{4,8},{5,9},{6,10},{7,11},{8,12},{9,13},{1... | collective-permute-start | bytes 6291464 | tf_op jit(solution)/shard_map/ppermute | solution.py:22
  233.3 26.0 %copy-start.19 = (bf16[512,1024]{1,0:T(8,128)(2,1)S(1)}, bf16[512,1024]{1,0:T(8,128)(2,1)}, u32[]{:S(2)}) copy-start(bf16[512,1024]{1,0:T(8,128)(2,1)} %param.16) | copy-start | bytes 3145732
  275.8 137.9 %collective-permute-start.4 = (bf16[2,2,2,2,128,1024]{5,4,0,1,2,3:T(8,128)(2,1)}, bf16[2,2,2,2,128,1024]{5,4,0,1,2,3:T(8,128)(2,1)}, u32[]{:S(2)}, u32[]{:S(2)}) collective-permute-start(bf16[2,2,2,2,128,1024]{5,4,0,1,2,3:T(8,128)(2,1)} %bitcast.253), channel_id=1, source_target_pairs={{0,1},{1,0},{2,3},{3,2},{4,5},{5,4},{6,7},{7,6},{8,9},{9,8},{10,11... | collective-permute-start | bytes 12582920 | tf_op jit(solution)/shard_map/ppermute | solution.py:76
  306.1 115.1 %collective-permute-start.5 = (bf16[2,2,2,2,32,4096]{5,4,0,3,1,2:T(8,128)(2,1)}, bf16[2,2,2,2,32,4096]{5,4,0,3,1,2:T(8,128)(2,1)}, u32[]{:S(2)}, u32[]{:S(2)}) collective-permute-start(bf16[2,2,2,2,32,4096]{5,4,0,3,1,2:T(8,128)(2,1)} %bitcast.252), channel_id=1, source_target_pairs={{0,1},{1,0},{2,3},{3,2},{4,5},{5,4},{6,7},{7,6},{8,9},{9,8},{10,11... | collective-permute-start | bytes 12582920 | tf_op jit(solution)/shard_map/ppermute | solution.py:76
  313.9 10.2 %copy-start.38 = (bf16[512,4096]{1,0:T(8,128)(2,1)S(1)}, bf16[512,4096]{1,0:T(8,128)(2,1)}, u32[]{:S(2)}) copy-start(bf16[512,4096]{1,0:T(8,128)(2,1)} %copy-done.37) | copy-start | bytes 12582916
  313.9 93.4 %collective-permute-start.9 = (bf16[512,2048]{1,0:T(8,128)(2,1)S(1)}, bf16[512,2048]{1,0:T(8,128)(2,1)S(1)}, u32[]{:S(2)}, u32[]{:S(2)}) collective-permute-start(bf16[512,2048]{1,0:T(8,128)(2,1)S(1)} %pad_maximum_fusion.1), channel_id=1, source_target_pairs={{0,1},{1,2},{2,3},{3,4},{4,5},{5,6},{6,7},{7,8},{8,9},{9,10},{10,1... | collective-permute-start | bytes 6291464 | tf_op jit(solution)/shard_map/ppermute | solution.py:22
  316.2 48.0 %collective-permute-start.7 = (bf16[512,2048]{1,0:T(8,128)(2,1)S(1)}, bf16[512,2048]{1,0:T(8,128)(2,1)S(1)}, u32[]{:S(2)}, u32[]{:S(2)}) collective-permute-start(bf16[512,2048]{1,0:T(8,128)(2,1)S(1)} %pad_maximum_fusion.1), channel_id=1, source_target_pairs={{0,3},{1,4},{2,5},{3,6},{4,7},{5,8},{6,9},{7,10},{8,11},{9,12},{10... | collective-permute-start | bytes 6291464 | tf_op jit(solution)/shard_map/ppermute | solution.py:22
  321.4 85.5 %collective-permute-start.8 = (bf16[512,2048]{1,0:T(8,128)(2,1)S(1)}, bf16[512,2048]{1,0:T(8,128)(2,1)S(1)}, u32[]{:S(2)}, u32[]{:S(2)}) collective-permute-start(bf16[512,2048]{1,0:T(8,128)(2,1)S(1)} %pad_maximum_fusion.1), channel_id=1, source_target_pairs={{0,2},{1,3},{2,4},{3,5},{4,6},{5,7},{6,8},{7,9},{8,10},{9,11},{10,... | collective-permute-start | bytes 6291464 | tf_op jit(solution)/shard_map/ppermute | solution.py:22
  426.3 104.8 %copy-start.1 = (f32[2,2,2,2,32,4096]{5,4,0,3,1,2:T(8,128)}, f32[2,2,2,2,32,4096]{5,4,0,3,1,2:T(8,128)S(1)}, u32[]{:S(2)}) copy-start(f32[2,2,2,2,32,4096]{5,4,0,3,1,2:T(8,128)S(1)} %convert_add_fusion) | copy-start | bytes 25165828
  460.1 72.6 %collective-permute-start.10 = (bf16[2,512,1024]{2,1,0:T(8,128)(2,1)}, bf16[2,512,1024]{2,1,0:T(8,128)(2,1)S(1)}, u32[]{:S(2)}, u32[]{:S(2)}) collective-permute-start(bf16[2,512,1024]{2,1,0:T(8,128)(2,1)} %get-tuple-element.50), channel_id=1, source_target_pairs={{1,0},{2,1},{3,2},{4,3},{5,4},{6,5},{7,6},{8,7},{9,8},{10,9},{11,1... | collective-permute-start | bytes 6291464 | tf_op jit(solution)/shard_map/ppermute | solution.py:22
  461.4 92.0 %collective-permute-start.13 = (bf16[2,512,1024]{2,1,0:T(8,128)(2,1)}, bf16[2,512,1024]{2,1,0:T(8,128)(2,1)S(1)}, u32[]{:S(2)}, u32[]{:S(2)}) collective-permute-start(bf16[2,512,1024]{2,1,0:T(8,128)(2,1)} %get-tuple-element.51), channel_id=1, source_target_pairs={{4,0},{5,1},{6,2},{7,3},{8,4},{9,5},{10,6},{11,7},{12,8},{13,9},{1... | collective-permute-start | bytes 6291464 | tf_op jit(solution)/shard_map/ppermute | solution.py:22
  462.7 90.7 %collective-permute-start.12 = (bf16[2,512,1024]{2,1,0:T(8,128)(2,1)}, bf16[2,512,1024]{2,1,0:T(8,128)(2,1)S(1)}, u32[]{:S(2)}, u32[]{:S(2)}) collective-permute-start(bf16[2,512,1024]{2,1,0:T(8,128)(2,1)} %get-tuple-element.52), channel_id=1, source_target_pairs={{3,0},{4,1},{5,2},{6,3},{7,4},{8,5},{9,6},{10,7},{11,8},{12,9},{13... | collective-permute-start | bytes 6291464 | tf_op jit(solution)/shard_map/ppermute | solution.py:22
  464.0 131.0 %collective-permute-start.11 = (bf16[2,512,1024]{2,1,0:T(8,128)(2,1)}, bf16[2,512,1024]{2,1,0:T(8,128)(2,1)}, u32[]{:S(2)}, u32[]{:S(2)}) collective-permute-start(bf16[2,512,1024]{2,1,0:T(8,128)(2,1)} %get-tuple-element.53), channel_id=1, source_target_pairs={{2,0},{3,1},{4,2},{5,3},{6,4},{7,5},{8,6},{9,7},{10,8},{11,9},{12,... | collective-permute-start | bytes 6291464 | tf_op jit(solution)/shard_map/ppermute | solution.py:22
  476.2 47.2 %copy-start.20 = (bf16[512,1024]{1,0:T(8,128)(2,1)S(1)}, bf16[512,1024]{1,0:T(8,128)(2,1)}, u32[]{:S(2)}) copy-start(bf16[512,1024]{1,0:T(8,128)(2,1)} %param.16) | copy-start | bytes 3145732
  480.2 156.1 %collective-permute-start.43 = (bf16[2,2,2,128,1024]{4,3,0,1,2:T(8,128)(2,1)}, bf16[2,2,2,128,1024]{4,3,0,1,2:T(8,128)(2,1)}, u32[]{:S(2)}, u32[]{:S(2)}) collective-permute-start(bf16[2,2,2,128,1024]{4,3,0,1,2:T(8,128)(2,1)} %fusion.54), channel_id=1, source_target_pairs={{0,2},{1,3},{2,0},{3,1},{4,6},{5,7},{6,4},{7,5},{8,10},{9,11},{10,... | collective-permute-start | bytes 6291464 | tf_op jit(solution)/shard_map/ppermute | solution.py:76
  532.7 128.4 %collective-permute-start.39 = (bf16[2,2,2,32,4096]{4,3,0,2,1:T(8,128)(2,1)}, bf16[2,2,2,32,4096]{4,3,0,2,1:T(8,128)(2,1)}, u32[]{:S(2)}, u32[]{:S(2)}) collective-permute-start(bf16[2,2,2,32,4096]{4,3,0,2,1:T(8,128)(2,1)} %fusion.53), channel_id=1, source_target_pairs={{0,4},{1,5},{2,6},{3,7},{4,0},{5,1},{6,2},{7,3},{8,12},{9,13},{10,... | collective-permute-start | bytes 6291464 | tf_op jit(solution)/shard_map/ppermute | solution.py:76
  622.3 42.6 %collective-permute-start.29 = (f32[2,2,2,2,1,384]{5,4,3,2,1,0:T(1,128)S(1)}, f32[2,2,2,2,1,384]{5,4,3,2,1,0:T(1,128)S(1)}, u32[]{:S(2)}, u32[]{:S(2)}) collective-permute-start(f32[2,2,2,2,1,384]{5,4,3,2,1,0:T(1,128)S(1)} %dynamic-slice_bitcast_fusion), channel_id=1, source_target_pairs={{0,1},{1,0},{2,3},{3,2},{4,5},{5,4},{6,7},{7,6},{8,9},{9,8},{10,11... | collective-permute-start | bytes 73736 | tf_op jit(solution)/shard_map/ppermute | solution.py:76
  622.4 38.7 %slice-start = ((s8[8388608]{0:T(1024)(128)(4,1)}), s8[4194304]{0:T(1024)(128)(4,1)S(1)}, s32[]{:S(2)}) async-start(s8[8388608]{0:T(1024)(128)(4,1)} %bitcast.259), calls=%async_computation.1 | async-start | bytes 8388608
  623.8 16.0 %copy-start.3 = (f32[2,512,1024]{2,1,0:T(8,128)S(1)}, f32[2,512,1024]{2,1,0:T(8,128)}, u32[]{:S(2)}) copy-start(f32[2,512,1024]{2,1,0:T(8,128)} %copy-done.2) | copy-start | bytes 12582916
  623.8 37.3 %slice-start.1 = ((s8[8388608]{0:T(1024)(128)(4,1)}), s8[4194304]{0:T(1024)(128)(4,1)S(1)}, s32[]{:S(2)}) async-start(s8[8388608]{0:T(1024)(128)(4,1)} %bitcast.259), calls=%async_computation.2 | async-start | bytes 8388608
  665.0 118.8 %copy-start.16 = (bf16[1024,1024]{1,0:T(8,128)(2,1)S(1)}, bf16[1024,1024]{1,0:T(8,128)(2,1)}, u32[]{:S(2)}) copy-start(bf16[1024,1024]{1,0:T(8,128)(2,1)} %convolution_convert_fusion.2) | copy-start | bytes 6291460
  665.0 77.7 %collective-permute-start.30 = (f32[2,2,2,1,384]{4,3,2,1,0:T(1,128)S(1)}, f32[2,2,2,1,384]{4,3,2,1,0:T(1,128)S(1)}, u32[]{:S(2)}, u32[]{:S(2)}) collective-permute-start(f32[2,2,2,1,384]{4,3,2,1,0:T(1,128)S(1)} %fusion.108), channel_id=1, source_target_pairs={{0,2},{1,3},{2,0},{3,1},{4,6},{5,7},{6,4},{7,5},{8,10},{9,11},{10,... | collective-permute-start | bytes 36872 | tf_op jit(solution)/shard_map/ppermute | solution.py:76
  740.1 51.4 %collective-permute-start.44 = (bf16[2,2,128,1024]{3,2,0,1:T(8,128)(2,1)S(1)}, bf16[2,2,128,1024]{3,2,0,1:T(8,128)(2,1)S(1)}, u32[]{:S(2)}, u32[]{:S(2)}) collective-permute-start(bf16[2,2,128,1024]{3,2,0,1:T(8,128)(2,1)S(1)} %fusion.81), channel_id=1, source_target_pairs={{0,4},{1,5},{2,6},{3,7},{4,0},{5,1},{6,2},{7,3},{8,12},{9,13},{10,... | collective-permute-start | bytes 3145736 | tf_op jit(solution)/shard_map/ppermute | solution.py:76
  742.7 23.1 %collective-permute-start.31 = (f32[2,2,1,384]{3,2,1,0:T(1,128)S(1)}, f32[2,2,1,384]{3,2,1,0:T(1,128)S(1)}, u32[]{:S(2)}, u32[]{:S(2)}) collective-permute-start(f32[2,2,1,384]{3,2,1,0:T(1,128)S(1)} %fusion.111), channel_id=1, source_target_pairs={{0,4},{1,5},{2,6},{3,7},{4,0},{5,1},{6,2},{7,3},{8,12},{9,13},{10,... | collective-permute-start | bytes 18440 | tf_op jit(solution)/shard_map/ppermute | solution.py:76
  744.3 48.1 %collective-permute-start.40 = (bf16[2,2,32,4096]{3,2,0,1:T(8,128)(2,1)S(1)}, bf16[2,2,32,4096]{3,2,0,1:T(8,128)(2,1)S(1)}, u32[]{:S(2)}, u32[]{:S(2)}) collective-permute-start(bf16[2,2,32,4096]{3,2,0,1:T(8,128)(2,1)S(1)} %fusion.80), channel_id=1, source_target_pairs={{0,8},{1,9},{2,10},{3,11},{4,12},{5,13},{6,14},{7,15},{8,0},{9,1},... | collective-permute-start | bytes 3145736 | tf_op jit(solution)/shard_map/ppermute | solution.py:76
  765.9 19.5 %collective-permute-start.32 = (f32[2,1,384]{2,1,0:T(1,128)S(1)}, f32[2,1,384]{2,1,0:T(1,128)S(1)}, u32[]{:S(2)}, u32[]{:S(2)}) collective-permute-start(f32[2,1,384]{2,1,0:T(1,128)S(1)} %fusion.114), channel_id=1, source_target_pairs={{0,8},{1,9},{2,10},{3,11},{4,12},{5,13},{6,14},{7,15},{8,0},{9,1},... | collective-permute-start | bytes 9224 | tf_op jit(solution)/shard_map/ppermute | solution.py:76
  784.6 10.2 %collective-permute-start.24 = (bf16[2,2,2,2,32,1024]{5,4,0,2,3,1:T(8,128)(2,1)S(1)}, bf16[2,2,2,2,32,1024]{5,4,0,2,3,1:T(8,128)(2,1)S(1)}, u32[]{:S(2)}, u32[]{:S(2)}) collective-permute-start(bf16[2,2,2,2,32,1024]{5,4,0,2,3,1:T(8,128)(2,1)S(1)} %bitcast.272), channel_id=1, source_target_pairs={{0,1},{1,0},{2,3},{3,2},{4,5},{5,4},{6,7},{7,6},{8,9},{9,8},{10,11... | collective-permute-start | bytes 3145736 | tf_op jit(solution)/shard_map/ppermute | solution.py:76
  784.7 11.0 %collective-permute-start.34 = (bf16[2,2,2,2,32,1024]{5,4,0,2,3,1:T(8,128)(2,1)S(1)}, bf16[2,2,2,2,32,1024]{5,4,0,2,3,1:T(8,128)(2,1)S(1)}, u32[]{:S(2)}, u32[]{:S(2)}) collective-permute-start(bf16[2,2,2,2,32,1024]{5,4,0,2,3,1:T(8,128)(2,1)S(1)} %bitcast.270), channel_id=1, source_target_pairs={{0,1},{1,0},{2,3},{3,2},{4,5},{5,4},{6,7},{7,6},{8,9},{9,8},{10,11... | collective-permute-start | bytes 3145736 | tf_op jit(solution)/shard_map/ppermute | solution.py:76
  785.4 4.5 collective-permute-start.33
  789.9 6.3 collective-permute-start.14
  790.5 81.0 %copy-start.36 = (f32[32]{0:T(128)}, f32[32]{0:T(128)S(1)}, u32[]{:S(2)}) copy-start(f32[32]{0:T(128)S(1)} %get-tuple-element.129) | copy-start | bytes 388
  791.6 7.3 collective-permute-start.19
  792.5 14.8 %collective-permute-start.45 = (bf16[2,128,1024]{2,1,0:T(8,128)(2,1)S(1)}, bf16[2,128,1024]{2,1,0:T(8,128)(2,1)S(1)}, u32[]{:S(2)}, u32[]{:S(2)}) collective-permute-start(bf16[2,128,1024]{2,1,0:T(8,128)(2,1)S(1)} %fusion.88), channel_id=1, source_target_pairs={{0,8},{1,9},{2,10},{3,11},{4,12},{5,13},{6,14},{7,15},{8,0},{9,1},... | collective-permute-start | bytes 1572872 | tf_op jit(solution)/shard_map/ppermute | solution.py:76
  794.9 14.9 %collective-permute-start.41 = (bf16[2,32,4096]{2,1,0:T(8,128)(2,1)S(1)}, bf16[2,32,4096]{2,1,0:T(8,128)(2,1)S(1)}, u32[]{:S(2)}, u32[]{:S(2)}) collective-permute-start(bf16[2,32,4096]{2,1,0:T(8,128)(2,1)S(1)} %fusion.87), channel_id=1, source_target_pairs={{0,2},{1,3},{2,0},{3,1},{4,6},{5,7},{6,4},{7,5},{8,10},{9,11},{10,... | collective-permute-start | bytes 1572872 | tf_op jit(solution)/shard_map/ppermute | solution.py:76
  795.7 28.4 %collective-permute-start.25 = (bf16[2,2,2,32,1024]{4,3,0,1,2:T(8,128)(2,1)S(1)}, bf16[2,2,2,32,1024]{4,3,0,1,2:T(8,128)(2,1)S(1)}, u32[]{:S(2)}, u32[]{:S(2)}) collective-permute-start(bf16[2,2,2,32,1024]{4,3,0,1,2:T(8,128)(2,1)S(1)} %fusion.85), channel_id=1, source_target_pairs={{0,8},{1,9},{2,10},{3,11},{4,12},{5,13},{6,14},{7,15},{8,0},{9,1},... | collective-permute-start | bytes 1572872 | tf_op jit(solution)/shard_map/ppermute | solution.py:76
  796.3 42.3 %collective-permute-start.35 = (bf16[2,2,2,32,1024]{4,3,0,1,2:T(8,128)(2,1)S(1)}, bf16[2,2,2,32,1024]{4,3,0,1,2:T(8,128)(2,1)S(1)}, u32[]{:S(2)}, u32[]{:S(2)}) collective-permute-start(bf16[2,2,2,32,1024]{4,3,0,1,2:T(8,128)(2,1)S(1)} %fusion.86), channel_id=1, source_target_pairs={{0,8},{1,9},{2,10},{3,11},{4,12},{5,13},{6,14},{7,15},{8,0},{9,1},... | collective-permute-start | bytes 1572872 | tf_op jit(solution)/shard_map/ppermute | solution.py:76
  798.9 40.2 %collective-permute-start.15 = (bf16[2,2,2,32,1024]{4,3,0,1,2:T(8,128)(2,1)S(1)}, bf16[2,2,2,32,1024]{4,3,0,1,2:T(8,128)(2,1)S(1)}, u32[]{:S(2)}, u32[]{:S(2)}) collective-permute-start(bf16[2,2,2,32,1024]{4,3,0,1,2:T(8,128)(2,1)S(1)} %fusion.83), channel_id=1, source_target_pairs={{0,2},{1,3},{2,0},{3,1},{4,6},{5,7},{6,4},{7,5},{8,10},{9,11},{10,... | collective-permute-start | bytes 1572872 | tf_op jit(solution)/shard_map/ppermute | solution.py:76
  807.3 33.7 %collective-permute-start.20 = (bf16[2,2,2,32,1024]{4,3,0,2,1:T(8,128)(2,1)S(1)}, bf16[2,2,2,32,1024]{4,3,0,2,1:T(8,128)(2,1)S(1)}, u32[]{:S(2)}, u32[]{:S(2)}) collective-permute-start(bf16[2,2,2,32,1024]{4,3,0,2,1:T(8,128)(2,1)S(1)} %fusion.84), channel_id=1, source_target_pairs={{0,4},{1,5},{2,6},{3,7},{4,0},{5,1},{6,2},{7,3},{8,12},{9,13},{10,... | collective-permute-start | bytes 1572872 | tf_op jit(solution)/shard_map/ppermute | solution.py:76
  809.7 45.8 %collective-permute-start.46 = (bf16[128,1024]{1,0:T(8,128)(2,1)S(1)}, bf16[128,1024]{1,0:T(8,128)(2,1)S(1)}, u32[]{:S(2)}, u32[]{:S(2)}) collective-permute-start(bf16[128,1024]{1,0:T(8,128)(2,1)S(1)} %fusion.94), channel_id=1, source_target_pairs={{0,16},{1,17},{2,18},{3,19},{4,20},{5,21},{6,22},{7,23},{8,24},{9,... | collective-permute-start | bytes 786440 | tf_op jit(solution)/shard_map/ppermute | solution.py:76
  824.1 30.2 %collective-permute-start.42 = (bf16[32,4096]{1,0:T(8,128)(2,1)S(1)}, bf16[32,4096]{1,0:T(8,128)(2,1)S(1)}, u32[]{:S(2)}, u32[]{:S(2)}) collective-permute-start(bf16[32,4096]{1,0:T(8,128)(2,1)S(1)} %fusion.93), channel_id=1, source_target_pairs={{0,16},{1,17},{2,18},{3,19},{4,20},{5,21},{6,22},{7,23},{8,24},{9,... | collective-permute-start | bytes 786440 | tf_op jit(solution)/shard_map/ppermute | solution.py:76
  838.5 9.2 %collective-permute-start.26 = (bf16[2,2,32,1024]{3,2,0,1:T(8,128)(2,1)S(1)}, bf16[2,2,32,1024]{3,2,0,1:T(8,128)(2,1)S(1)}, u32[]{:S(2)}, u32[]{:S(2)}) collective-permute-start(bf16[2,2,32,1024]{3,2,0,1:T(8,128)(2,1)S(1)} %fusion.91), channel_id=1, source_target_pairs={{0,2},{1,3},{2,0},{3,1},{4,6},{5,7},{6,4},{7,5},{8,10},{9,11},{10,... | collective-permute-start | bytes 786440 | tf_op jit(solution)/shard_map/ppermute | solution.py:76
  839.0 12.8 %collective-permute-start.36 = (bf16[2,2,32,1024]{3,2,0,1:T(8,128)(2,1)S(1)}, bf16[2,2,32,1024]{3,2,0,1:T(8,128)(2,1)S(1)}, u32[]{:S(2)}, u32[]{:S(2)}) collective-permute-start(bf16[2,2,32,1024]{3,2,0,1:T(8,128)(2,1)S(1)} %fusion.92), channel_id=1, source_target_pairs={{0,2},{1,3},{2,0},{3,1},{4,6},{5,7},{6,4},{7,5},{8,10},{9,11},{10,... | collective-permute-start | bytes 786440 | tf_op jit(solution)/shard_map/ppermute | solution.py:76
  841.0 11.2 %collective-permute-start.16 = (bf16[2,2,32,1024]{3,2,0,1:T(8,128)(2,1)S(1)}, bf16[2,2,32,1024]{3,2,0,1:T(8,128)(2,1)S(1)}, u32[]{:S(2)}, u32[]{:S(2)}) collective-permute-start(bf16[2,2,32,1024]{3,2,0,1:T(8,128)(2,1)S(1)} %fusion.89), channel_id=1, source_target_pairs={{0,4},{1,5},{2,6},{3,7},{4,0},{5,1},{6,2},{7,3},{8,12},{9,13},{10,... | collective-permute-start | bytes 786440 | tf_op jit(solution)/shard_map/ppermute | solution.py:76
  847.8 6.4 collective-permute-start.21
  851.8 5.4 collective-permute-start.27
  852.3 7.3 collective-permute-start.37
  854.2 6.2 collective-permute-start.17
  854.4 8.4 collective-permute-start.22
  857.3 9.5 %collective-permute-start.28 = (bf16[32,1024]{1,0:T(8,128)(2,1)S(1)}, bf16[32,1024]{1,0:T(8,128)(2,1)S(1)}, u32[]{:S(2)}, u32[]{:S(2)}) collective-permute-start(bf16[32,1024]{1,0:T(8,128)(2,1)S(1)} %fusion.101), channel_id=1, source_target_pairs={{0,16},{1,17},{2,18},{3,19},{4,20},{5,21},{6,22},{7,23},{8,24},{9,... | collective-permute-start | bytes 196616 | tf_op jit(solution)/shard_map/ppermute | solution.py:76
  859.6 11.3 %collective-permute-start.38 = (bf16[32,1024]{1,0:T(8,128)(2,1)S(1)}, bf16[32,1024]{1,0:T(8,128)(2,1)S(1)}, u32[]{:S(2)}, u32[]{:S(2)}) collective-permute-start(bf16[32,1024]{1,0:T(8,128)(2,1)S(1)} %fusion.102), channel_id=1, source_target_pairs={{0,16},{1,17},{2,18},{3,19},{4,20},{5,21},{6,22},{7,23},{8,24},{9,... | collective-permute-start | bytes 196616 | tf_op jit(solution)/shard_map/ppermute | solution.py:76
  860.4 9.0 %collective-permute-start.18 = (bf16[32,1024]{1,0:T(8,128)(2,1)S(1)}, bf16[32,1024]{1,0:T(8,128)(2,1)S(1)}, u32[]{:S(2)}, u32[]{:S(2)}) collective-permute-start(bf16[32,1024]{1,0:T(8,128)(2,1)S(1)} %fusion.99), channel_id=1, source_target_pairs={{0,16},{1,17},{2,18},{3,19},{4,20},{5,21},{6,22},{7,23},{8,24},{9,... | collective-permute-start | bytes 196616 | tf_op jit(solution)/shard_map/ppermute | solution.py:76
  862.8 7.3 collective-permute-start.23
  (26 other events, 99.3 us)
Sparse Core Ops, SparseCore 0:
  18.4 158.6 all-gather.1
